TPU v7x, 32 devices: a whole 2x2x4 slice. The times are simulated.
32 devices in a mesh: dp: 32 (over z, y, x, core).
Axes of the slice: x: 2, y: 2, z: 4, core: 2. Of those that a mesh axis runs over, the one named last changes fastest.
Arguments:
- block_in: bfloat16 [65536, 256], P('dp'), may hold values from -6 to 6
- lengths: int32 [64], P('dp'), may hold values from 204 to 1024, as said below
- back_w: bfloat16 [512, 256], P('dp'), may hold values from -0.25 to 0.25
- back_b: bfloat16 [256], P('dp'), may hold values from -3 to 3
- heads_w: bfloat16 [256, 768], P('dp'), may hold values from -0.375 to 0.375
- heads_b: bfloat16 [768], P('dp'), may hold values from -5 to 2
- norm1_gain: bfloat16 [256], P('dp'), may hold values from 0.099609375 to 1.8984375
- norm1_bias: bfloat16 [256], P('dp'), may hold values from -2.5 to 2.5
- norm2_gain: bfloat16 [256], P('dp'), may hold values from 0.099609375 to 1.8984375
- norm2_bias: bfloat16 [256], P('dp'), may hold values from -2.5 to 2.5
- up_w: bfloat16 [256, 1024], P('dp'), may hold values from -0.375 to 0.375
- up_b: bfloat16 [1024], P('dp'), may hold values from -3 to 3
- down_w: bfloat16 [1024, 256], P('dp'), may hold values from -0.375 to 0.375
- down_b: bfloat16 [256], P('dp'), may hold values from -2.5 to 2.5
- cotangent: bfloat16 [65536, 256], P('dp'), may hold values from -6 to 6
Outputs:
- block_out: bfloat16 [65536, 256], P('dp')
- input_grad: bfloat16 [65536, 256], P('dp')
- backward_weight_gradient: float32 [512, 256], P('dp')
- grad_back_b: float32 [256], P('dp')
- grad_heads_w: float32 [256, 768], P('dp')
- grad_heads_b: float32 [768], P('dp')
- grad_norm1_gain: float32 [256], P('dp')
- grad_norm1_bias: float32 [256], P('dp')
- grad_norm2_gain: float32 [256], P('dp')
- grad_norm2_bias: float32 [256], P('dp')
- grad_up_w: float32 [256, 1024], P('dp')
- grad_up_b: float32 [1024], P('dp')
- grad_down_w: float32 [1024, 256], P('dp')
- grad_down_b: float32 [256], P('dp')
Inputs may be any that keep to these rules, and one draw needn't show every extreme that they name: `lengths`: one sequence has exactly 1024 live steps in every draw.
All inputs are finite; a program needn't handle non-finite values.
Results may differ from a plain program's by a relative error of at most 0.0063.
Values may be sent and summed in bfloat16 or wider, within the bound.
A program may use at most 128 MiB of HBM per device.

v0:
```python
import jax
import jax.numpy as jnp
from jax import lax
from jax.sharding import PartitionSpec as P

SPAN = 64


def lecun_tanh(values):
    return 1.7159 * jnp.tanh(0.666 * values)


def lecun_slope(values):
    inner = jnp.tanh(0.666 * values)
    return 1.7159 * 0.666 * (1.0 - inner * inner)


def layer_norm(values, norm_gain, norm_shift):
    row_mean = jnp.mean(values, axis=-1, keepdims=True)
    centered = values - row_mean
    variance = jnp.mean(centered * centered, axis=-1, keepdims=True)
    return centered * lax.rsqrt(variance + 1e-05) * norm_gain + norm_shift


def block_scan(running_state, pieces):
    log_keep, forcing_term = pieces
    block_len = log_keep.shape[1]
    summed_logarithm = jnp.cumsum(log_keep, axis=1)
    log_ratio = summed_logarithm[:, :, None, :] - summed_logarithm[:, None, :, :]
    causal = (jnp.arange(block_len)[:, None] >= jnp.arange(block_len)[None, :])[None, :, :, None]
    weight_tree = jnp.where(causal, jnp.exp(jnp.where(causal, log_ratio, 0.0)), 0.0)
    final_output = (
        jnp.einsum("enfp,efp->enp", weight_tree, forcing_term)
        + jnp.exp(summed_logarithm) * running_state[:, None, :]
    )
    return (final_output[:, -1, :], final_output)


def run_blocks(log_keep, forcing_term):
    seq_count, length, model_width = log_keep.shape
    block_count = length // SPAN
    shaped = (seq_count, block_count, SPAN, model_width)
    keep_blocks = log_keep.reshape(shaped).transpose(1, 0, 2, 3)
    drive_blocks = forcing_term.reshape(shaped).transpose(1, 0, 2, 3)
    start = jnp.zeros((seq_count, model_width), jnp.float32)
    final_state, states = lax.scan(jax.checkpoint(block_scan), start, (keep_blocks, drive_blocks))
    return states.transpose(1, 0, 2, 3).reshape(seq_count, length, model_width)


def cell_tail(pre_heads, norm_gain, norm_shift, validity):
    model_width = norm_gain.shape[0]
    rate = pre_heads[..., :model_width]
    value_head = jnp.tanh(pre_heads[..., model_width : 2 * model_width])
    fallback = jnp.tanh(pre_heads[..., 2 * model_width :])
    opened = jax.nn.sigmoid(rate)
    log_keep = jnp.log1p(-validity * opened)
    forcing_term = validity * (opened * value_head + (1.0 - opened) * fallback)
    states = run_blocks(log_keep, forcing_term)
    return validity * layer_norm(states, norm_gain, norm_shift)


def product(left, right):
    return jnp.dot(left, right, preferred_element_type=jnp.float32)


def outer_sum(left, right):
    return lax.dot_general(
        left, right, (((0,), (0,)), ((), ())), preferred_element_type=jnp.float32
    )


def back_product(left, right):
    return lax.dot_general(
        left, right, (((1,), (1,)), ((), ())), preferred_element_type=jnp.float32
    )


def column_sums(values):
    return jnp.sum(values.astype(jnp.float32), axis=0)


def local(
    block_in,
    lengths,
    back_w,
    back_b,
    heads_w,
    heads_b,
    norm1_gain,
    norm1_bias,
    norm2_gain,
    norm2_bias,
    up_w,
    up_b,
    down_w,
    down_b,
    cotangent,
):
    seq_count = lengths.shape[0]
    length = block_in.shape[0] // seq_count
    model_width = block_in.shape[1]
    positions = jnp.arange(length, dtype=jnp.int32)
    validity = (positions[None, :] < lengths[:, None]).astype(jnp.float32)[:, :, None]
    row_valid = validity.reshape(seq_count * length, 1)
    shaped_in = block_in.reshape(seq_count, length, model_width)
    previous = jnp.concatenate(
        [jnp.zeros_like(shaped_in[:, :1]), shaped_in[:, :-1]], axis=1
    ).reshape(seq_count * length, model_width)
    cell_set = (back_w, back_b, heads_w, heads_b, norm1_gain, norm1_bias)
    mlp_set = (norm2_gain, norm2_bias, up_w, up_b, down_w, down_b)
    cell_full = (
        lax.all_gather(cell_set[0], "dp", axis=0, tiled=True),
        lax.all_gather(cell_set[1], "dp", axis=0, tiled=True),
        lax.all_gather(cell_set[2], "dp", axis=0, tiled=True),
        lax.all_gather(cell_set[3], "dp", axis=0, tiled=True),
        lax.all_gather(cell_set[4], "dp", axis=0, tiled=True),
        lax.all_gather(cell_set[5], "dp", axis=0, tiled=True),
    )
    full_back_w, full_back_b, full_heads_w, full_heads_b, full_gain_one, full_bias_one = cell_full
    pre_back = (
        product(block_in, full_back_w[:model_width])
        + product(previous, full_back_w[model_width:])
        + full_back_b.astype(jnp.float32)
    )
    features = lecun_tanh(pre_back).astype(jnp.bfloat16)
    pre_heads = product(features, full_heads_w) + full_heads_b.astype(jnp.float32)

    def cell_branch(head_values, norm_gain, norm_shift):
        shaped_heads = head_values.reshape(seq_count, length, 3 * model_width)
        return cell_tail(shaped_heads, norm_gain, norm_shift, validity).reshape(
            seq_count * length, model_width
        )

    branch_one, tail_pull = jax.vjp(
        cell_branch, pre_heads, full_gain_one.astype(jnp.float32), full_bias_one.astype(jnp.float32)
    )
    mid = block_in.astype(jnp.float32) + branch_one
    mlp_full = (
        lax.all_gather(mlp_set[0], "dp", axis=0, tiled=True),
        lax.all_gather(mlp_set[1], "dp", axis=0, tiled=True),
        lax.all_gather(mlp_set[2], "dp", axis=0, tiled=True),
        lax.all_gather(mlp_set[3], "dp", axis=0, tiled=True),
        lax.all_gather(mlp_set[4], "dp", axis=0, tiled=True),
        lax.all_gather(mlp_set[5], "dp", axis=0, tiled=True),
    )
    full_gain_two, full_bias_two, full_up_w, full_up_b, full_down_w, full_down_b = mlp_full
    normed_f32, norm_pull = jax.vjp(
        layer_norm, mid, full_gain_two.astype(jnp.float32), full_bias_two.astype(jnp.float32)
    )
    normed = normed_f32.astype(jnp.bfloat16)
    pre_up = product(normed, full_up_w) + full_up_b.astype(jnp.float32)

    def smooth(values):
        return jax.nn.gelu(values, approximate=True)

    hidden_f32, gelu_pull = jax.vjp(smooth, pre_up)
    hidden = hidden_f32.astype(jnp.bfloat16)
    branch_two = product(hidden, full_down_w) + full_down_b.astype(jnp.float32)
    block_out = (mid + row_valid * branch_two).astype(jnp.bfloat16)
    mlp_full = (
        lax.all_gather(mlp_set[0], "dp", axis=0, tiled=True),
        lax.all_gather(mlp_set[1], "dp", axis=0, tiled=True),
        lax.all_gather(mlp_set[2], "dp", axis=0, tiled=True),
        lax.all_gather(mlp_set[3], "dp", axis=0, tiled=True),
        lax.all_gather(mlp_set[4], "dp", axis=0, tiled=True),
        lax.all_gather(mlp_set[5], "dp", axis=0, tiled=True),
    )
    back_gain_two, back_bias_two, back_up_w, back_up_b, back_down_w, back_down_b = mlp_full
    output_gradient = cotangent * row_valid.astype(jnp.bfloat16)
    grad_down_w = outer_sum(hidden, output_gradient)
    grad_down_b = column_sums(output_gradient)
    grad_hidden = back_product(output_gradient, back_down_w)
    grad_pre_up = gelu_pull(grad_hidden)[0].astype(jnp.bfloat16)
    grad_up_w = outer_sum(normed, grad_pre_up)
    grad_up_b = column_sums(grad_pre_up)
    grad_normed = back_product(grad_pre_up, back_up_w)
    grad_mid_norm, grad_gain_two, grad_bias_two = norm_pull(grad_normed)
    grad_mid = cotangent.astype(jnp.float32) + grad_mid_norm
    mlp_grads = (grad_gain_two, grad_bias_two, grad_up_w, grad_up_b, grad_down_w, grad_down_b)
    mlp_owned = (
        lax.psum_scatter(mlp_grads[0], "dp", scatter_dimension=0, tiled=True),
        lax.psum_scatter(mlp_grads[1], "dp", scatter_dimension=0, tiled=True),
        lax.psum_scatter(mlp_grads[2], "dp", scatter_dimension=0, tiled=True),
        lax.psum_scatter(mlp_grads[3], "dp", scatter_dimension=0, tiled=True),
        lax.psum_scatter(mlp_grads[4], "dp", scatter_dimension=0, tiled=True),
        lax.psum_scatter(mlp_grads[5], "dp", scatter_dimension=0, tiled=True),
    )
    cell_full = (
        lax.all_gather(cell_set[0], "dp", axis=0, tiled=True),
        lax.all_gather(cell_set[1], "dp", axis=0, tiled=True),
        lax.all_gather(cell_set[2], "dp", axis=0, tiled=True),
        lax.all_gather(cell_set[3], "dp", axis=0, tiled=True),
        lax.all_gather(cell_set[4], "dp", axis=0, tiled=True),
        lax.all_gather(cell_set[5], "dp", axis=0, tiled=True),
    )
    back_back_w, back_back_b, back_heads_w, back_heads_b, back_gain_one, back_bias_one = cell_full
    grad_pre_heads_f32, grad_gain_one, grad_bias_one = tail_pull(grad_mid)
    grad_pre_heads = grad_pre_heads_f32.astype(jnp.bfloat16)
    grad_heads_w = outer_sum(features, grad_pre_heads)
    grad_heads_b = column_sums(grad_pre_heads)
    grad_features = back_product(grad_pre_heads, back_heads_w)
    grad_pre_back = (grad_features * lecun_slope(pre_back)).astype(jnp.bfloat16)
    backward_weight_gradient = jnp.concatenate(
        [outer_sum(block_in, grad_pre_back), outer_sum(previous, grad_pre_back)], axis=0
    )
    grad_back_b = column_sums(grad_pre_back)
    grad_current = back_product(grad_pre_back, back_back_w[:model_width])
    grad_previous = back_product(grad_pre_back, back_back_w[model_width:]).reshape(
        seq_count, length, model_width
    )
    moved_up = jnp.concatenate(
        [grad_previous[:, 1:], jnp.zeros_like(grad_previous[:, :1])], axis=1
    ).reshape(seq_count * length, model_width)
    input_grad = (grad_mid + grad_current + moved_up).astype(jnp.bfloat16)
    cell_grads = (
        backward_weight_gradient,
        grad_back_b,
        grad_heads_w,
        grad_heads_b,
        grad_gain_one,
        grad_bias_one,
    )
    cell_owned = (
        lax.psum_scatter(cell_grads[0], "dp", scatter_dimension=0, tiled=True),
        lax.psum_scatter(cell_grads[1], "dp", scatter_dimension=0, tiled=True),
        lax.psum_scatter(cell_grads[2], "dp", scatter_dimension=0, tiled=True),
        lax.psum_scatter(cell_grads[3], "dp", scatter_dimension=0, tiled=True),
        lax.psum_scatter(cell_grads[4], "dp", scatter_dimension=0, tiled=True),
        lax.psum_scatter(cell_grads[5], "dp", scatter_dimension=0, tiled=True),
    )
    return (
        block_out,
        input_grad,
        cell_owned[0],
        cell_owned[1],
        cell_owned[2],
        cell_owned[3],
        cell_owned[4],
        cell_owned[5],
        mlp_owned[0],
        mlp_owned[1],
        mlp_owned[2],
        mlp_owned[3],
        mlp_owned[4],
        mlp_owned[5],
    )


def solution(mesh):
    return jax.shard_map(
        local,
        mesh=mesh,
        in_specs=(
            P("dp", None),
            P("dp"),
            P("dp", None),
            P("dp"),
            P("dp", None),
            P("dp"),
            P("dp"),
            P("dp"),
            P("dp"),
            P("dp"),
            P("dp", None),
            P("dp"),
            P("dp", None),
            P("dp"),
            P("dp", None),
        ),
        out_specs=(
            P("dp", None),
            P("dp", None),
            P("dp", None),
            P("dp"),
            P("dp", None),
            P("dp"),
            P("dp"),
            P("dp"),
            P("dp"),
            P("dp"),
            P("dp", None),
            P("dp"),
            P("dp", None),
            P("dp"),
        ),
        check_vma=False,
    )
```

profile of v0, /device:TPU:0, one launch (start us, length us, event | category | flops | bytes accessed | tf_op | source)
XLA Modules:
  0.0 1155.9 jit_solution(11456720487846057257)
XLA Ops:
  16.8 42.1 %all-reduce.23 = (bf16[768]{0:T(1024)(128)(2,1)S(1)}, bf16[256]{0:T(256)(128)(2,1)S(1)}, bf16[256]{0:T(256)(128)(2,1)}, bf16[256]{0:T(256)(128)(2,1)}, bf16[256]...) all-reduce(bf16[768]{0:T(1024)(128)(2,1)S(1)} %dynamic-update-slice, ...), channel_id=1, replica_groups=mesh['dp'=32] {'dp'}, use_global_device_ids=true, to_apply=%add.7 | all-reduce | flops 3328 | bytes 13312
  58.9 41.4 %all_gather.40 = bf16[512,256]{1,0:T(8,128)(2,1)S(1)} all-gather(bf16[16,256]{1,0:T(8,128)(2,1)} %param.21), channel_id=1, replica_groups=mesh['dp'=32] {'dp'}, dimensions={0}, use_global_device_ids=true | all-gather | bytes 270336 | tf_op jit(solution)/shard_map/all_gather | solution.py:112
  100.3 37.9 %all_gather.42 = bf16[256,768]{1,0:T(8,128)(2,1)S(1)} all-gather(bf16[8,768]{1,0:T(8,128)(2,1)} %param.23), channel_id=1, replica_groups=mesh['dp'=32] {'dp'}, dimensions={0}, use_global_device_ids=true | all-gather | bytes 405504 | tf_op jit(solution)/shard_map/all_gather | solution.py:114
  148.8 98.4 %while.37 = (s32[]{:T(128)}, f32[2,256]{1,0:T(2,128)S(1)}, f32[16,2,64,256]{3,2,1,0:T(8,128)S(1)}, f32[16,2,256]{2,1,0:T(2,128)}, f32[16,2,64,256]{3,2,1,0:T(8,1...) while((s32[]{:T(128)}, f32[2,256]{1,0:T(2,128)S(1)}, ...), condition=%wide.region_2.3_spmd.clone.clone, body=%wide.region_0.2_spmd.clone.clone.sunk | while | flops 12582914 | bytes 1722985 | solution.py:46
  150.6 3.7 multiply_reduce_fusion.13
  156.7 3.7 multiply_reduce_fusion.13
  162.9 3.7 multiply_reduce_fusion.13
  169.0 3.7 multiply_reduce_fusion.13
  175.2 3.7 multiply_reduce_fusion.13
  181.3 3.7 multiply_reduce_fusion.13
  187.5 3.7 multiply_reduce_fusion.13
  193.6 3.7 multiply_reduce_fusion.13
  199.7 3.7 multiply_reduce_fusion.13
  205.9 3.7 multiply_reduce_fusion.13
  212.0 3.7 multiply_reduce_fusion.13
  218.2 3.7 multiply_reduce_fusion.13
  224.3 3.7 multiply_reduce_fusion.13
  253.7 39.4 %all_gather.48 = bf16[256,1024]{1,0:T(8,128)(2,1)S(1)} all-gather(bf16[8,1024]{1,0:T(8,128)(2,1)S(1)} %copy-done.32), channel_id=1, replica_groups=mesh['dp'=32] {'dp'}, dimensions={0}, use_global_device_ids=true | all-gather | bytes 540672 | tf_op jit(solution)/shard_map/all_gather | solution.py:141
  293.1 38.0 %all_gather.50 = bf16[1024,256]{1,0:T(8,128)(2,1)S(1)} all-gather(bf16[32,256]{1,0:T(8,128)(2,1)S(1)} %copy-done.33), channel_id=1, replica_groups=mesh['dp'=32] {'dp'}, dimensions={0}, use_global_device_ids=true | all-gather | bytes 540672 | tf_op jit(solution)/shard_map/all_gather | solution.py:143
  331.2 5.2 multiply_convert_fusion
  336.4 8.2 convert_reduce_fusion
  355.6 4.6 fusion.27
  363.9 274.2 %while.36 = (s32[]{:T(128)}, f32[2,256]{1,0:T(2,128)}, f32[16,2,64,256]{3,2,0,1:T(8,128)}, f32[16,2,64,256]{3,2,0,1:T(8,128)}, f32[16,2,256]{2,1,0:T(2,128)}, /*...) while((s32[]{:T(128)}, f32[2,256]{1,0:T(2,128)}, ...), condition=%wide.region_17.18_spmd, body=%wide.region_11.17_spmd.sunk | while | flops 31591940 | bytes 4878541 | solution.py:46
  369.5 4.0 multiply_reduce_fusion.12
  373.5 4.1 fusion.83
  386.7 4.0 multiply_reduce_fusion.12
  390.7 4.1 fusion.83
  403.8 4.0 multiply_reduce_fusion.12
  407.9 4.1 fusion.83
  421.0 4.0 multiply_reduce_fusion.12
  425.0 4.1 fusion.83
  438.1 4.0 multiply_reduce_fusion.12
  442.1 4.1 fusion.83
  455.3 4.0 multiply_reduce_fusion.12
  459.3 4.1 fusion.83
  472.4 4.0 multiply_reduce_fusion.12
  476.4 4.1 fusion.83
  489.5 4.0 multiply_reduce_fusion.12
  493.5 4.1 fusion.83
  506.6 4.0 multiply_reduce_fusion.12
  510.7 4.1 fusion.83
  523.8 4.0 multiply_reduce_fusion.12
  527.8 4.1 fusion.83
  540.9 4.0 multiply_reduce_fusion.12
  544.9 4.1 fusion.83
  558.1 4.0 multiply_reduce_fusion.12
  562.1 4.1 fusion.83
  575.2 4.0 multiply_reduce_fusion.12
  579.2 4.1 fusion.83
  592.3 4.0 multiply_reduce_fusion.12
  596.3 4.1 fusion.83
  609.5 4.0 multiply_reduce_fusion.12
  613.5 4.1 fusion.83
  626.6 4.0 multiply_reduce_fusion.12
  630.6 4.1 fusion.83
  638.1 5.3 fusion.24
  648.7 4.4 fusion.39
  653.2 5.7 fusion.54
  659.0 5.2 fusion.34
  664.4 37.2 %all-reduce.22 = (f32[256]{0:T(256)S(1)}, f32[768]{0:T(1024)S(1)}, f32[256]{0:T(256)S(1)}, f32[256]{0:T(256)S(1)}, f32[256]{0:T(256)S(1)}, /*index=5*/f32[256]{0:T(256)S(1)}, f32[1024]{0:T(1024)S(1)}, f32[256]{0:T(256)S(1)}) all-reduce(f32[256]{0:T(256)S(1)} %get-tuple-element.458, ...), channel_id=3, replica_groups=mesh['dp'=32] {'dp'}, use_global_device_ids=true, to_apply=%region_20.21.clone | all-reduce | flops 3328 | bytes 26624
  713.0 67.3 %reduce-scatter.5.cloned.1.call-done = f32[16,256]{1,0:T(8,128)} async-done(((f32[512,256]{1,0:T(8,128)}), f32[16,256]{1,0:T(8,128)}) %reduce-scatter.5.cloned.1.call-update) | async-done | bytes 16400 | tf_op jit(solution)/shard_map/reduce_scatter | solution.py:224
  780.3 98.1 %reduce-scatter.7.cloned.1.call-done = f32[8,768]{1,0:T(8,128)} async-done(((f32[256,768]{1,0:T(8,128)}), f32[8,768]{1,0:T(8,128)}) %reduce-scatter.7.cloned.1.call-update) | async-done | bytes 24592 | tf_op jit(solution)/shard_map/reduce_scatter | solution.py:226
  878.3 137.2 %reduce-scatter.9.cloned.1.call-done = f32[8,1024]{1,0:T(8,128)} async-done(((f32[256,1024]{1,0:T(8,128)}), f32[8,1024]{1,0:T(8,128)}) %reduce-scatter.9.cloned.1.call-update) | async-done | bytes 32784 | tf_op jit(solution)/shard_map/reduce_scatter | solution.py:183
  1015.5 133.8 %reduce-scatter.11.cloned.1.call-done = f32[32,256]{1,0:T(8,128)} async-done(((f32[1024,256]{1,0:T(8,128)}), f32[32,256]{1,0:T(8,128)}) %reduce-scatter.11.cloned.1.call-update) | async-done | bytes 32784 | tf_op jit(solution)/shard_map/reduce_scatter | solution.py:185
  (539 shorter events, 251.4 us)
Async XLA Ops:
  7.2 132.8 %copy-start.8 = (bf16[2048,256]{1,0:T(8,128)(2,1)S(1)}, bf16[2048,256]{1,0:T(8,128)(2,1)}, u32[]{:S(2)}) copy-start(bf16[2048,256]{1,0:T(8,128)(2,1)} %param.19) | copy-start | bytes 3145732
  7.2 773.1 %reduce-scatter.5.cloned.1.call-start = ((), (), s32[]{:S(2)}) async-start(), calls=%async_computation.4 | async-start | bytes 540672 | tf_op jit(solution)/shard_map/reduce_scatter | solution.py:224
  9.4 133.7 %copy-start.22 = (f32[2,1024]{1,0:T(2,128)}, f32[2,1024]{1,0:T(2,128)S(1)}, u32[]{:S(2)}) copy-start(f32[2,1024]{1,0:T(2,128)S(1)} %fusion.48) | copy-start | bytes 24580
  100.3 40.0 %copy-start.15 = (bf16[512,256]{1,0:T(8,128)(2,1)}, bf16[512,256]{1,0:T(8,128)(2,1)S(1)}, u32[]{:S(2)}) copy-start(bf16[512,256]{1,0:T(8,128)(2,1)S(1)} %all_gather.40) | copy-start | bytes 786436
  138.2 3.5 copy-start.17
  247.9 104.3 %copy-start.23 = (f32[1,8,2,128]{3,1,2,0:T(8,128)}, f32[1,8,2,128]{3,1,2,0:T(8,128)S(1)}, u32[]{:S(2)}) copy-start(f32[1,8,2,128]{3,1,2,0:T(8,128)S(1)} %copy.146) | copy-start | bytes 24580
  247.9 100.7 %copy-start.30 = (bf16[1,8,2,128]{3,1,2,0:T(8,128)(2,1)}, bf16[1,8,2,128]{3,1,2,0:T(8,128)(2,1)S(1)}, u32[]{:S(2)}) copy-start(bf16[1,8,2,128]{3,1,2,0:T(8,128)(2,1)S(1)} %copy.147) | copy-start | bytes 12292
  252.8 94.3 %copy-start.5 = (f32[2048,256]{1,0:T(8,128)}, f32[2048,256]{1,0:T(8,128)S(1)}, u32[]{:S(2)}) copy-start(f32[2048,256]{1,0:T(8,128)S(1)} %get-tuple-element.435) | copy-start | bytes 6291460
  252.9 40.3 %copy-start.33 = (bf16[32,256]{1,0:T(8,128)(2,1)S(1)}, bf16[32,256]{1,0:T(8,128)(2,1)}, u32[]{:S(2)}) copy-start(bf16[32,256]{1,0:T(8,128)(2,1)} %param.31) | copy-start | bytes 49156
  252.9 94.2 %copy-start.25 = (f32[2048]{0:T(1024)}, f32[2048]{0:T(1024)S(1)}, u32[]{:S(2)}) copy-start(f32[2048]{0:T(1024)S(1)} %broadcast_multiply_fusion) | copy-start | bytes 24580
  253.5 93.6 %copy-start.28 = (f32[2048]{0:T(1024)}, f32[2048]{0:T(1024)S(1)}, u32[]{:S(2)}) copy-start(f32[2048]{0:T(1024)S(1)} %fusion.47) | copy-start | bytes 24580
  253.6 93.5 %copy-start.42 = (f32[256]{0:T(256)}, f32[256]{0:T(256)S(1)}, u32[]{:S(2)}) copy-start(f32[256]{0:T(256)S(1)} %convert_element_type.115) | copy-start | bytes 3076
  253.7 82.7 %copy-start.49 = (f32[256]{0:T(256)}, f32[256]{0:T(256)S(1)}, u32[]{:S(2)}) copy-start(f32[256]{0:T(256)S(1)} %convert_element_type.116) | copy-start | bytes 3076
  331.2 5.2 copy-start.20
  331.2 5.2 copy-start.19
  369.5 4.0 copy-start.13
  369.5 4.0 copy-start.14
  386.7 4.0 copy-start.13
  386.7 4.0 copy-start.14
  403.8 4.0 copy-start.13
  403.8 4.0 copy-start.14
  420.9 4.0 copy-start.13
  420.9 4.0 copy-start.14
  438.1 4.0 copy-start.13
  438.1 4.0 copy-start.14
  455.2 4.0 copy-start.13
  455.2 4.0 copy-start.14
  472.4 4.0 copy-start.13
  472.4 4.0 copy-start.14
  489.5 4.0 copy-start.13
  489.5 4.0 copy-start.14
  506.6 4.0 copy-start.13
  506.6 4.0 copy-start.14
  523.8 4.0 copy-start.13
  523.8 4.0 copy-start.14
  540.9 4.0 copy-start.13
  540.9 4.0 copy-start.14
  558.0 4.0 copy-start.13
  558.0 4.0 copy-start.14
  575.2 4.0 copy-start.13
  575.2 4.0 copy-start.14
  592.3 4.0 copy-start.13
  592.3 4.0 copy-start.14
  609.4 4.0 copy-start.13
  609.4 4.0 copy-start.14
  626.6 4.0 copy-start.13
  626.6 4.0 copy-start.14
  648.6 4.6 copy-start.26
  648.6 4.6 copy-start.29
  648.6 4.6 copy-start.43
  648.6 4.6 copy-start.50
  648.6 229.7 %reduce-scatter.7.cloned.1.call-start = ((), (), s32[]{:S(2)}) async-start(), calls=%async_computation.5 | async-start | bytes 811008 | tf_op jit(solution)/shard_map/reduce_scatter | solution.py:226
  653.1 5.8 copy-start.31
  653.1 362.4 %reduce-scatter.9.cloned.1.call-start = ((), (), s32[]{:S(2)}) async-start(), calls=%async_computation.6 | async-start | bytes 1081344 | tf_op jit(solution)/shard_map/reduce_scatter | solution.py:183
  658.9 490.4 %reduce-scatter.11.cloned.1.call-start = ((), (), s32[]{:S(2)}) async-start(), calls=%async_computation.7 | async-start | bytes 1081344 | tf_op jit(solution)/shard_map/reduce_scatter | solution.py:185
  659.0 5.3 copy-start.35
  659.0 5.3 copy-start.36
  659.0 5.3 copy-start.37
  659.0 5.3 copy-start.38
  659.0 5.3 copy-start.40
  659.0 5.3 copy-start.41
  659.0 46.0 %copy-start.10 = (bf16[2048,256]{1,0:T(8,128)(2,1)S(1)}, bf16[2048,256]{1,0:T(8,128)(2,1)}, u32[]{:S(2)}) copy-start(bf16[2048,256]{1,0:T(8,128)(2,1)} %copy-done.9) | copy-start | bytes 3145732
  659.0 46.0 %copy-start.16 = (bf16[512,256]{1,0:T(8,128)(2,1)S(1)}, bf16[512,256]{1,0:T(8,128)(2,1)}, u32[]{:S(2)}) copy-start(bf16[512,256]{1,0:T(8,128)(2,1)} %copy-done.15) | copy-start | bytes 786436
  707.5 3.2 copy-start.21
  (23 other events, 35.9 us)
Sparse Core Ops, SparseCore 0:
  648.7 131.5 reduce-scatter.4
  786.8 91.5 reduce-scatter.6
  881.3 134.2 reduce-scatter.8
  1018.2 131.0 reduce-scatter.10
where the time goes:
time: 1160 us
  waiting for transfers between devices  436 us (38%)
  other arithmetic  262 us (23%)
  blocking collectives  236 us (20%)
  local copies, waits for them, and re-layouts  165 us (14%)
  matrix products  40.7 us (4%)
  between operations  14.5 us (1%)
    reduce_scatter x1, waiting for transfers between devices, local(): lax.psum_scatter(mlp_grads[2], 'dp', scatter_dimension=0, tiled=True)  137 us
    reduce_scatter x1, waiting for transfers between devices, local(): lax.psum_scatter(mlp_grads[4], 'dp', scatter_dimension=0, tiled=True)  134 us
    dot_general x32, other arithmetic, block_scan(): jnp.einsum('enfp,efp->enp', weight_tree, forcing_term)  124 us
    reduce_scatter x1, waiting for transfers between devices, local(): lax.psum_scatter(cell_grads[2], 'dp', scatter_dimension=0, tiled=True)  98.1 us
    squeeze x80, local copies, waits for them, and re-layouts, run_blocks(): lax.scan(jax.checkpoint(block_scan), start, (keep_blocks, drive_blocks))  91.5 us
    unnamed x2, blocking collectives  79.3 us
    reduce_scatter x1, waiting for transfers between devices, local(): lax.psum_scatter(cell_grads[0], 'dp', scatter_dimension=0, tiled=True)  67.3 us
    reduce_sum x16, other arithmetic, block_scan(): summed_logarithm[:, :, None, :] - summed_logarithm[:, None, :, :]  65.4 us
  transfers between devices with their start and end apart: 4, of which 4 were waited for; matrix products, arithmetic and copies ran while one was open for 2% of the time, Pallas kernels for 0%

commit v1 on v0

v1 whole, which is shorter than its diff:
```python
import functools
import jax
import jax.numpy as jnp
from jax import lax
from jax.experimental import pallas as pl
from jax.experimental.pallas import tpu as pltpu
from jax.sharding import PartitionSpec as P

BLK = 256
LANES = 8
STEPS = BLK // LANES
QUAD = 4
FF_STEP = 256
F32 = jnp.float32
BF16 = jnp.bfloat16
MESH = pl.DeviceIdType.MESH
GC = 0.7978845608028654
GA = 0.044715


def mm(a, b):
    return lax.dot_general(a, b, (((1,), (0,)), ((), ())), preferred_element_type=F32)


def mm_nt(a, b):
    return lax.dot_general(a, b, (((1,), (1,)), ((), ())), preferred_element_type=F32)


def mm_tn(a, b):
    return lax.dot_general(a, b, (((0,), (0,)), ((), ())), preferred_element_type=F32)


def shuffle(transposed=False):
    row = lax.broadcasted_iota(jnp.int32, (BLK, BLK), 0)
    col = lax.broadcasted_iota(jnp.int32, (BLK, BLK), 1)
    if transposed:
        row, col = col, row
    return jnp.where((row & 7) * STEPS + (row >> 3) == col, 1.0, 0.0).astype(BF16)


def fold(values):
    return jnp.sum(values.reshape(values.shape[0] // 8, 8, values.shape[1]), axis=0)


def sublane(shape):
    return lax.broadcasted_iota(jnp.int32, shape, 0)


def flat(ref):
    values = ref[...]
    return values.reshape(-1, values.shape[-1])


def block_rows(i, dims):
    return pl.ds(i * (dims[0] * BLK), dims[0] * BLK)


def enter(i, r, dims):
    S, L, D = dims
    order = shuffle()
    sub = sublane((8, D))
    joined = []
    for s in range(S):
        mixed = mm(order, r.x[pl.ds(s * L + i * BLK, BLK), :])
        turned = pltpu.roll(mixed[BLK - 8 :], 1, 0)
        first = jnp.where(sub == 0, jnp.where(i == 0, 0.0, r.xcarry[s]), turned)
        r.xcarry[s] = turned
        before = jnp.concatenate([first, mixed[: BLK - 8]], axis=0)
        joined.append(jnp.concatenate([mixed, before], axis=1))
    r.joined[block_rows(i, dims), :] = jnp.concatenate(joined, axis=0).astype(BF16)


def backbone(i, r, dims):
    rows = block_rows(i, dims)
    inner = jnp.tanh(0.666 * (mm(r.joined[rows, :], flat(r.wb)) + r.bb[...]))
    r.inner[rows, :] = inner
    r.feat[rows, :] = (1.7159 * inner).astype(BF16)


def gates(i, r, dims):
    S, L, D = dims
    rows = block_rows(i, dims)
    sub = sublane((8, D))
    heads = mm(r.feat[rows, :], r.wh[...]) + r.bh[...]
    o = 0.5 * jnp.tanh(0.5 * heads[:, :D]) + 0.5
    v = jnp.tanh(heads[:, D : 2 * D])
    f = jnp.tanh(heads[:, 2 * D :])
    r.o[rows, :] = o
    r.v[rows, :] = v
    r.f[rows, :] = f
    keep = 1.0 - o
    drive = f + o * (v - f)
    one = jnp.ones((8, D), F32)
    for s in range(S):
        k = [keep[s * BLK + 8 * j : s * BLK + 8 * j + 8] for j in range(STEPS)]
        d = [drive[s * BLK + 8 * j : s * BLK + 8 * j + 8] for j in range(STEPS)]
        A, Q = k[0], d[0]
        for j in range(1, STEPS):
            Q = k[j] * Q + d[j]
            A = k[j] * A
        for sh in (1, 2, 4):
            An = jnp.where(sub < sh, one, pltpu.roll(A, sh, 0))
            Qn = jnp.where(sub < sh, 0.0, pltpu.roll(Q, sh, 0))
            Q = Q + A * Qn
            A = A * An
        carry = jnp.where(i == 0, 0.0, r.scarry[s])
        ends = Q + A * carry
        start = jnp.where(sub == 0, carry, pltpu.roll(ends, 1, 0))
        r.scarry[s] = jnp.broadcast_to(ends[7:8], (8, D))
        r.start[i, s] = start
        Q = start
        for j in range(STEPS):
            Q = k[j] * Q + d[j]
            r.state[pl.ds(i * (S * BLK) + s * BLK + 8 * j, 8), :] = Q


def live(i, r, dims):
    S, L, D = dims
    row = lax.broadcasted_iota(jnp.int32, (BLK, D), 0)
    time = (row & 7) * STEPS + (row >> 3) + i * BLK
    return jnp.concatenate([time < r.lengths[s] for s in range(S)], axis=0)


def normalise(values, D):
    mean = jnp.sum(values, axis=1, keepdims=True) * (1.0 / D)
    c = values - mean
    var = jnp.sum(c * c, axis=1, keepdims=True) * (1.0 / D)
    rs = lax.rsqrt(var + 1e-05)
    return c * rs, rs


def norm_back(dy, gain, xhat, rs, D):
    dx = dy * gain
    m1 = jnp.sum(dx, axis=1, keepdims=True) * (1.0 / D)
    m2 = jnp.sum(dx * xhat, axis=1, keepdims=True) * (1.0 / D)
    return rs * (dx - m1 - xhat * m2)


def feed_forward(i, r, dims):
    S, L, D = dims
    FF = r.wu.shape[1]
    rows = block_rows(i, dims)
    order, back = shuffle(), shuffle(True)
    valid = live(i, r, dims)
    g1, b1, g2, b2 = r.g1[...], r.b1[...], r.g2[...], r.b2[...]
    xhat1, rs1 = normalise(r.state[rows, :], D)
    mid = r.joined[rows, pl.ds(0, D)].astype(F32) + jnp.where(valid, xhat1 * g1 + b1, 0.0)
    xhat2, rs2 = normalise(mid, D)
    normed = (xhat2 * g2 + b2).astype(BF16)
    r.normed[rows, :] = normed
    cot = jnp.concatenate([mm(order, r.cot[pl.ds(s * L + i * BLK, BLK), :]) for s in range(S)], axis=0)
    gout32 = jnp.where(valid, cot, 0.0)
    r.gbd[...] += fold(gout32)
    gout = gout32.astype(BF16)
    r.gout[rows, :] = gout
    W = FF_STEP
    y = gn = None
    for n in range(FF // W):
        cols = slice(n * W, (n + 1) * W)
        down = r.wd_rows(n, W)
        pu = mm(normed, r.wu[:, cols]) + r.bu[:, cols]
        v2 = pu * pu
        h = 0.5 * jnp.tanh(pu * (v2 * (GC * GA) + GC)) + 0.5
        hid = pu * h
        hid16 = hid.astype(BF16)
        r.hidden[rows, cols] = hid16
        slope = h + hid * (1.0 - h) * (v2 * (6.0 * GA * GC) + 2.0 * GC)
        gpu = (mm_nt(gout, down) * slope).astype(BF16)
        r.gpu[rows, cols] = gpu
        r.gbu[:, cols] += fold(gpu.astype(F32))
        yn = mm(hid16, down)
        gnn = mm_nt(gpu, r.wu[:, cols])
        y = yn if y is None else y + yn
        gn = gnn if gn is None else gn + gnn
    out = (mid + jnp.where(valid, y + r.bd[...], 0.0)).astype(BF16)
    for s in range(S):
        r.out[pl.ds(s * L + i * BLK, BLK), :] = mm(back, out[s * BLK : (s + 1) * BLK]).astype(BF16)
    r.gg2[...] += fold(gn * xhat2)
    r.gb2[...] += fold(gn)
    gmid = cot + norm_back(gn, g2, xhat2, rs2, D)
    r.gmid[rows, :] = gmid
    dy1 = jnp.where(valid, gmid, 0.0)
    r.gg1[...] += fold(dy1 * xhat1)
    r.gb1[...] += fold(dy1)
    r.gnorm[rows, :] = norm_back(dy1, g1, xhat1, rs1, D)


def gates_back(i, r, dims):
    S, L, D = dims
    nb = L // BLK
    rows = block_rows(i, dims)
    sub = sublane((8, D))
    o = r.o[rows, :]
    keep = 1.0 - o
    gnorm = r.gnorm[rows, :]
    state = r.state[rows, :]
    gss, sps = [], []
    one = jnp.ones((8, D), F32)
    for s in range(S):
        k = [keep[s * BLK + 8 * j : s * BLK + 8 * j + 8] for j in range(STEPS)]
        g = [gnorm[s * BLK + 8 * j : s * BLK + 8 * j + 8] for j in range(STEPS)]
        A = k[STEPS - 1]
        H = k[STEPS - 1] * g[STEPS - 1]
        for j in range(STEPS - 2, -1, -1):
            H = k[j] * (g[j] + H)
            A = k[j] * A
        for sh in (1, 2, 4):
            An = jnp.where(sub >= 8 - sh, one, pltpu.roll(A, 8 - sh, 0))
            Hn = jnp.where(sub >= 8 - sh, 0.0, pltpu.roll(H, 8 - sh, 0))
            H = H + A * Hn
            A = A * An
        carry = jnp.where(i == nb - 1, 0.0, r.scarry[s])
        ends = H + A * carry
        r.scarry[s] = jnp.broadcast_to(ends[0:1], (8, D))
        H = jnp.where(sub == 7, carry, pltpu.roll(ends, 7, 0))
        out = [None] * STEPS
        for j in range(STEPS - 1, -1, -1):
            G = g[j] + H
            H = k[j] * G
            out[j] = G
        gss += out
        sps += [r.start[i, s], state[s * BLK : (s + 1) * BLK - 8]]
    gs = jnp.concatenate(gss, axis=0)
    sp = jnp.concatenate(sps, axis=0)
    v = r.v[rows, :]
    f = r.f[rows, :]
    go = gs * o
    grate = go * keep * (v - f - sp)
    gv = go * (1.0 - v * v)
    gf = (gs - go) * (1.0 - f * f)
    gph = jnp.concatenate([grate, gv, gf], axis=1).astype(BF16)
    r.gph[rows, :] = gph
    r.gbh[...] += fold(gph.astype(F32))
    inner = r.inner[rows, :]
    gpb = (mm_nt(gph, r.wh[...]) * ((1.7159 * 0.666) * (1.0 - inner * inner))).astype(BF16)
    r.gpb[rows, :] = gpb
    r.gbb[...] += fold(gpb.astype(F32))


def leave(i, r, dims):
    S, L, D = dims
    nb = L // BLK
    rows = block_rows(i, dims)
    sub = sublane((8, D))
    back = shuffle(True)
    gj = mm_nt(r.gpb[rows, :], flat(r.wb))
    gmid = r.gmid[rows, :]
    for s in range(S):
        own = gj[s * BLK : (s + 1) * BLK, :D]
        before = gj[s * BLK : (s + 1) * BLK, D:]
        turned = pltpu.roll(before[:8], 7, 0)
        last = jnp.where(sub == 7, jnp.where(i == nb - 1, 0.0, r.xcarry[s]), turned)
        r.xcarry[s] = turned
        moved = jnp.concatenate([before[8:], last], axis=0)
        grad = (gmid[s * BLK : (s + 1) * BLK] + own + moved).astype(BF16)
        r.ig[pl.ds(s * L + i * BLK, BLK), :] = mm(back, grad).astype(BF16)


SUMS = ("gbb", "gbh", "gg1", "gb1", "gg2", "gb2", "gbu", "gbd")


def zero_sums(r):
    for name in SUMS:
        ref = getattr(r, name)
        ref[...] = jnp.zeros_like(ref)


def sum_widths(D, FF):
    return (D, 3 * D, D, D, D, D, FF, D)


def work_space(S, L, D, FF):
    T = S * L
    v = pltpu.VMEM
    space = dict(
        joined=v((T, 2 * D), BF16), inner=v((T, D), F32), feat=v((T, D), BF16),
        o=v((T, D), F32), v=v((T, D), F32), f=v((T, D), F32), state=v((T, D), F32),
        start=v((L // BLK, S, 8, D), F32), xcarry=v((S, 8, D), F32), scarry=v((S, 8, D), F32),
        normed=v((T, D), BF16), gout=v((T, D), BF16), hidden=v((T, FF), BF16), gpu=v((T, FF), BF16),
        gmid=v((T, D), F32), gnorm=v((T, D), F32), gph=v((T, 3 * D), BF16), gpb=v((T, D), BF16),
    )
    for name, width in zip(SUMS, sum_widths(D, FF)):
        space[name] = v((8, width), F32)
    return space


class Refs:
    def wd_rows(self, n, width):
        if len(self.wd.shape) == 2:
            return self.wd[pl.ds(n * width, width), :]
        z, q, c, piece, columns = self.wd.shape
        plane = q * c * piece
        return self.wd[pl.ds(n * width // plane, width // plane)].reshape(width, columns)


def refs_of(names, refs):
    r = Refs()
    for name, ref in zip(names, refs):
        setattr(r, name, ref)
    return r


class Place:
    def __init__(self, n):
        self.n = n
        self.planes = n // (2 * QUAD)
        self.me = lax.axis_index("dp")
        self.c = self.me % 2
        self.q = (self.me // 2) % QUAD
        self.z = self.me // (2 * QUAD)
        self.partner = self.me + 1 - 2 * self.c

    def plane(self, k):
        return (self.z + k) % self.planes

    def corner(self, k):
        return (self.q + k) % QUAD

    def device(self, z, q):
        return (z * QUAD + q) * 2 + self.c

    def others(self):
        return [(a, b) for a in range(self.planes) for b in range(QUAD) if a or b]


class Copies:
    def __init__(self, send, recv):
        self.send, self.recv, self.used, self.open = send, recv, 0, []

    def start(self, src, dst, device):
        k = self.used
        self.used += 1
        copy = pltpu.make_async_remote_copy(
            src_ref=src, dst_ref=dst, send_sem=self.send.at[k], recv_sem=self.recv.at[k],
            device_id=(device,), device_id_type=MESH,
        )
        copy.start()
        self.open.append(copy)
        return copy

    def finish(self):
        for copy in self.open:
            copy.wait_send()


def arrived(copies):
    for copy in copies:
        copy.wait_recv()


def cut(values):
    half = values.shape[-1] // 2
    return jnp.concatenate([values[..., :half], values[..., half:]], axis=-2)


def uncut(values):
    return jnp.concatenate([values[..., :8, :], values[..., 8:, :]], axis=-1)


def same(values):
    return values


class Share:
    def __init__(self, r, name, cutter, copies, place, direct):
        self.r, self.name, self.cut, self.copies, self.p, self.direct = r, name, cutter, copies, place, direct

    def ref(self, kind):
        return getattr(self.r, kind + self.name)

    def pair(self):
        p = self.p
        self.ref("cs")[...] = self.cut(self.ref("dw")[:, :, 1 - p.c]).astype(BF16)
        self.paired = self.copies.start(self.ref("cs"), self.ref("cr"), p.partner)

    def spread(self):
        p = self.p
        self.paired.wait_recv()
        total = self.cut(self.ref("dw")[:, :, p.c]) + self.ref("cr")[...].astype(F32)
        xs = self.ref("xs")
        xs[...] = total.astype(BF16)
        self.sent = []
        if self.direct:
            for k, (a, b) in enumerate(p.others()):
                z, q = p.plane(a), p.corner(b)
                self.sent.append(self.copies.start(xs.at[z, q], self.ref("xr").at[k], p.device(z, q)))
        else:
            for b in range(1, QUAD):
                q = p.corner(b)
                self.sent.append(self.copies.start(xs.at[:, q], self.ref("xr").at[b - 1], p.device(p.z, q)))

    def climb(self):
        p = self.p
        arrived(self.sent)
        acc = self.cut(self.ref("dw")[:, p.q, p.c]) + self.ref("cr")[:, p.q].astype(F32)
        for b in range(QUAD - 1):
            acc = acc + self.ref("xr")[b].astype(F32)
        self.ref("ac")[...] = acc
        self.ref("zs")[...] = acc.astype(BF16)
        self.sent = []
        for a in range(1, p.planes):
            z = p.plane(a)
            self.sent.append(self.copies.start(self.ref("zs").at[z], self.ref("zr").at[a - 1], p.device(z, p.q)))

    def land(self):
        p = self.p
        arrived(self.sent)
        if self.direct:
            acc = self.cut(self.ref("dw")[p.z, p.q, p.c]) + self.ref("cr")[p.z, p.q].astype(F32)
            for k in range(len(self.sent)):
                acc = acc + self.ref("xr")[k].astype(F32)
        else:
            acc = self.ref("ac")[p.z]
            for k in range(len(self.sent)):
                acc = acc + self.ref("zr")[k].astype(F32)
        return acc


def share_space(name, n, rows, columns, cutting, direct):
    Z, v = n // (2 * QUAD), pltpu.VMEM
    R, C = (2 * rows, columns // 2) if cutting else (rows, columns)
    space = {
        "dw" + name: v((Z, QUAD, 2, rows, columns), F32),
        "cs" + name: v((Z, QUAD, R, C), BF16),
        "cr" + name: v((Z, QUAD, R, C), BF16),
        "xs" + name: v((Z, QUAD, R, C), BF16),
    }
    if direct:
        space["xr" + name] = v((Z * QUAD - 1, R, C), BF16)
    else:
        space["xr" + name] = v((QUAD - 1, Z, R, C), BF16)
        space["ac" + name] = v((Z, R, C), F32)
        space["zs" + name] = v((Z, R, C), BF16)
        space["zr" + name] = v((Z - 1, R, C), BF16)
    return space


def segments(n, D, FF):
    found, lane, offset = [], 0, 0
    for name, width in zip(("bb", "bh", "g1", "b1", "g2", "b2", "bu", "bd"), sum_widths(D, FF)):
        found.append((name, lane, width, width // n, offset))
        lane, offset = lane + width, offset + width // n
    return found


def fill_pick(r, n, D, FF):
    for name, lane, width, own, offset in segments(n, D, FF):
        l = lax.broadcasted_iota(jnp.int32, (width, 128), 0).astype(F32)
        k = lax.broadcasted_iota(jnp.int32, (width, 128), 1).astype(F32)
        place = l - own * jnp.floor((l + 0.5) * (1.0 / own)) + offset
        r.pick[pl.ds(lane, width), :] = jnp.where(place == k, 1.0, 0.0).astype(BF16)


def owners(n, D, FF):
    parts = []
    for name, lane, width, own, offset in segments(n, D, FF):
        l = lax.broadcasted_iota(jnp.int32, (n, width), 1).astype(F32)
        row = lax.broadcasted_iota(jnp.int32, (n, width), 0)
        device = (2 * (row % (n // 2)) + row // (n // 2)).astype(F32)
        parts.append(jnp.floor((l + 0.5) * (1.0 / own)) == device)
    return jnp.concatenate(parts, axis=1)


ROWS = ("gback", "gheads", "gup", "gdown", "gvec")
INPUTS = ("lengths", "x_hbm", "cot_hbm", "wb_own", "wh_own", "wu_own", "wd_own", "vec_own")
OUTPUTS = ("out_hbm", "ig_hbm") + ROWS


def mega(names, dims, n, FF, *refs):
    r = refs_of(names, refs)
    S, L, D = dims
    nb = L // BLK
    p = Place(n)
    chips = n // 2
    chip = p.z * QUAD + p.q
    copies = Copies(r.send, r.recv)

    def run(f, first, last, down=False):
        def step(i, c):
            f(nb - 1 - i if down else i, r, dims)
            return c
        lax.fori_loop(first, last, step, 0)

    barrier = pltpu.get_barrier_semaphore()
    for a, b in p.others():
        pl.semaphore_signal(barrier, inc=1, device_id=(p.device(p.plane(a), p.corner(b)),), device_id_type=MESH)
    pl.semaphore_signal(barrier, inc=1, device_id=(p.partner,), device_id_type=MESH)

    loads = [
        pltpu.make_async_copy(src, dst, r.local.at[k])
        for k, (src, dst) in enumerate((
            (r.wb_own, r.wb.at[p.z, p.q, p.c]), (r.vec_own, r.vec.at[p.c, pl.ds(chip, 1)]),
            (r.wh_own, r.wh_mine), (r.wu_own, r.wu_mine), (r.wd_own, r.wd.at[p.z, p.q, p.c]),
            (r.x_hbm, r.x), (r.cot_hbm, r.cot),
        ))
    ]
    for load in loads:
        load.start()
    for load in loads[:5]:
        load.wait()
    r.wh_cut[p.z, p.q, p.c] = cut(r.wh_mine[...].astype(F32)).astype(BF16)
    r.wu_cut[p.z, p.q, p.c] = cut(r.wu_mine[...].astype(F32)).astype(BF16)
    pl.semaphore_wait(barrier, len(p.others()) + 1)

    def send_all(ref):
        return [
            copies.start(ref.at[p.z, p.q, p.c], ref.at[p.z, p.q, p.c], p.device(p.plane(a), p.corner(b)))
            for a, b in p.others()
        ]

    def send_planes(ref):
        return [
            copies.start(ref.at[p.z, p.q, p.c], ref.at[p.z, p.q, p.c], p.device(p.plane(a), p.q))
            for a in range(1, p.planes)
        ]

    def send_corners(ref):
        return [
            copies.start(ref.at[:, p.q, p.c], ref.at[:, p.q, p.c], p.device(p.z, p.corner(b)))
            for b in range(1, QUAD)
        ]

    def send_pair(ref):
        return [copies.start(ref.at[:, :, p.c], ref.at[:, :, p.c], p.partner)]

    wb_in = send_all(r.wb)
    vec_in = [
        copies.start(r.vec.at[p.c, pl.ds(chip, 1)], r.vec.at[p.c, pl.ds(chip, 1)], p.device(p.plane(a), p.corner(b)))
        for a, b in p.others()
    ]
    wh_in = send_all(r.wh_cut)
    up_in = send_planes(r.wu_cut)
    down_in = send_planes(r.wd)

    zero_sums(r)
    fill_pick(r, n, D, FF)
    loads[5].wait()
    run(enter, 0, nb)

    arrived(wb_in)
    wb_in = send_pair(r.wb)
    arrived(vec_in)
    vec_in = [copies.start(r.vec.at[p.c], r.vec.at[p.c], p.partner)]
    arrived(wb_in)
    arrived(vec_in)
    spread = mm_nt(r.vec[...].reshape(n, 128).astype(BF16), r.pick[...])
    vectors = jnp.sum(jnp.where(owners(n, D, FF), spread, 0.0), axis=0, keepdims=True)
    for name, lane, width, own, offset in segments(n, D, FF):
        getattr(r, name)[...] = vectors[:, lane : lane + width]

    run(backbone, 0, nb)
    arrived(wh_in)
    wh_in = send_pair(r.wh_cut)
    arrived(up_in)
    up_in = send_corners(r.wu_cut)
    arrived(down_in)
    down_in = send_corners(r.wd)
    arrived(wh_in)
    r.wh[...] = uncut(r.wh_cut[...].astype(F32)).reshape(D, 3 * D).astype(BF16)
    run(gates, 0, nb)
    arrived(up_in)
    up_in = send_pair(r.wu_cut)
    arrived(down_in)
    down_in = send_pair(r.wd)
    arrived(up_in)
    r.wu[...] = uncut(r.wu_cut[...].astype(F32)).reshape(D, FF).astype(BF16)
    arrived(down_in)
    loads[6].wait()
    run(feed_forward, 0, nb)
    outs = [pltpu.make_async_copy(r.out, r.out_hbm, r.local.at[7])]
    outs[0].start()

    up = Share(r, "u", cut, copies, p, False)
    down = Share(r, "d", same, copies, p, False)
    heads = Share(r, "h", cut, copies, p, True)
    back = Share(r, "b", same, copies, p, True)
    r.dwu[...] = mm_tn(r.normed[...], r.gpu[...]).reshape(r.dwu.shape)
    up.pair()
    r.dwd[...] = mm_tn(r.gout[...], r.hidden[...]).T.reshape(r.dwd.shape)
    down.pair()
    run(gates_back, 0, 1, True)
    up.spread()
    down.spread()
    run(gates_back, 1, nb - 1, True)
    up.climb()
    down.climb()
    run(gates_back, nb - 1, nb, True)
    r.dwh[...] = mm_tn(r.feat[...], r.gph[...]).reshape(r.dwh.shape)
    heads.pair()
    r.dwb[...] = mm_tn(r.gpb[...], r.joined[...]).T.reshape(r.dwb.shape)
    back.pair()

    sums = jnp.concatenate([jnp.sum(getattr(r, name)[...], axis=0, keepdims=True) for name in SUMS], axis=1)
    mine = owners(n, D, FF)
    rest, rows = jnp.where(mine, sums, 0.0), None
    for _ in range(3):
        part = rest.astype(BF16)
        rest = rest - part.astype(F32)
        row = mm(part, r.pick[...])
        rows = row if rows is None else rows + row
    r.vs[...] = rows.reshape(2, chips, 128)
    vec_pair = copies.start(r.vs.at[1 - p.c], r.vr, p.partner)
    run(leave, 0, 1, True)
    heads.spread()
    back.spread()
    vec_pair.wait_recv()
    r.va[...] = r.vs[p.c] + r.vr[...]
    vec_out = []
    for a, b in p.others():
        z, q = p.plane(a), p.corner(b)
        vec_out.append(copies.start(r.va.at[pl.ds(z * QUAD + q, 1)], r.vt.at[pl.ds(chip, 1)], p.device(z, q)))
    r.vt[pl.ds(chip, 1), :] = r.va[pl.ds(chip, 1), :]
    run(leave, 1, nb, True)
    outs.append(pltpu.make_async_copy(r.ig, r.ig_hbm, r.local.at[8]))
    outs[1].start()
    r.gup[...] = uncut(up.land())
    r.gdown[...] = down.land()
    r.gheads[...] = uncut(heads.land())
    r.gback[...] = back.land()
    arrived(vec_out)
    r.gvec[...] = jnp.sum(r.vt[...], axis=0, keepdims=True)
    copies.finish()
    for out in outs:
        out.wait()


def quick(lengths, x, cot, wb, wh, wu, wd, vectors, n):
    S = lengths.shape[0]
    T, D = x.shape
    L, FF = T // S, wu.shape[1]
    Z, chips, v = n // (2 * QUAD), n // 2, pltpu.VMEM
    space = work_space(S, L, D, FF)
    rb, rh, ru, rd = wb.shape[0], wh.shape[0], wu.shape[0], wd.shape[0]
    space.update(
        x=v((T, D), BF16), cot=v((T, D), BF16), out=v((T, D), BF16), ig=v((T, D), BF16),
        wb=v((Z, QUAD, 2, rb, D), BF16), wd=v((Z, QUAD, 2, rd, D), BF16),
        wh_cut=v((Z, QUAD, 2, 2 * rh, 3 * D // 2), BF16), wu_cut=v((Z, QUAD, 2, 2 * ru, FF // 2), BF16),
        wh=v((D, 3 * D), BF16), wu=v((D, FF), BF16), wh_mine=v((rh, 3 * D), BF16), wu_mine=v((ru, FF), BF16),
        vec=v((2, chips, 128), F32), pick=v((sum(sum_widths(D, FF)), 128), BF16),
        vs=v((2, chips, 128), F32), vr=v((chips, 128), F32), va=v((chips, 128), F32), vt=v((chips, 128), F32),
        local=pltpu.SemaphoreType.DMA((9,)), send=pltpu.SemaphoreType.DMA((160,)), recv=pltpu.SemaphoreType.DMA((160,)),
    )
    for name, lane, width, own, offset in segments(n, D, FF):
        space[name] = v((1, width), F32)
    space.update(share_space("u", n, ru, FF, True, False))
    space.update(share_space("d", n, rd, D, False, False))
    space.update(share_space("h", n, rh, 3 * D, True, True))
    space.update(share_space("b", n, rb, D, False, True))
    row = lambda a, b: jax.ShapeDtypeStruct((a, b), F32)
    shapes = (
        jax.ShapeDtypeStruct((T, D), BF16), jax.ShapeDtypeStruct((T, D), BF16),
        row(rb, D), row(rh, 3 * D), row(ru, FF), row(rd, D), row(1, 128),
    )
    hbm, vmem = pl.BlockSpec(memory_space=pl.ANY), pl.BlockSpec(memory_space=pltpu.VMEM)
    return pl.pallas_call(
        functools.partial(mega, INPUTS + OUTPUTS + tuple(space), (S, L, D), n, FF),
        out_shape=shapes,
        in_specs=[pl.BlockSpec(memory_space=pltpu.SMEM)] + [hbm] * 7,
        out_specs=[hbm, hbm] + [vmem] * 5,
        scratch_shapes=list(space.values()),
        compiler_params=pltpu.CompilerParams(collective_id=0, has_side_effects=True, vmem_limit_bytes=62 << 20),
    )(lengths, x, cot, wb, wh, wu, wd, vectors)


def plain(names, dims, *refs):
    r = refs_of(names, refs)
    S, L, D = dims
    nb = L // BLK

    def run(f, down=False):
        def step(i, c):
            f(nb - 1 - i if down else i, r, dims)
            return c
        lax.fori_loop(0, nb, step, 0)

    zero_sums(r)
    for f in (enter, backbone, gates, feed_forward):
        run(f)
    r.gup[...] = mm_tn(r.normed[...], r.gpu[...])
    r.gdown[...] = mm_tn(r.gout[...], r.hidden[...]).T
    run(gates_back, True)
    r.gheads[...] = mm_tn(r.feat[...], r.gph[...])
    r.gback[...] = mm_tn(r.gpb[...], r.joined[...]).T
    run(leave, True)
    for name in SUMS:
        getattr(r, "all" + name)[...] = jnp.sum(getattr(r, name)[...], axis=0, keepdims=True)


def whole(lengths, x, cot, matrices, vectors):
    S = lengths.shape[0]
    T, D = x.shape
    L, FF = T // S, matrices[2].shape[1]
    space = work_space(S, L, D, FF)
    names = ("lengths", "x", "cot", "wb", "wh", "wu", "wd", "bb", "bh", "g1", "b1", "g2", "b2", "bu", "bd")
    names += ("out", "ig") + ROWS[:4] + tuple("all" + name for name in SUMS) + tuple(space)
    row = lambda a, b: jax.ShapeDtypeStruct((a, b), F32)
    shapes = (jax.ShapeDtypeStruct((T, D), BF16),) * 2
    shapes += tuple(row(*m.shape) for m in matrices) + tuple(row(1, width) for width in sum_widths(D, FF))
    vmem = pl.BlockSpec(memory_space=pltpu.VMEM)
    return pl.pallas_call(
        functools.partial(plain, names, (S, L, D)),
        out_shape=shapes,
        in_specs=[pl.BlockSpec(memory_space=pltpu.SMEM)] + [vmem] * 14,
        out_specs=[vmem] * len(shapes),
        scratch_shapes=list(space.values()),
        compiler_params=pltpu.CompilerParams(vmem_limit_bytes=62 << 20),
    )(lengths, x, cot, *matrices, *(v.astype(F32).reshape(1, -1) for v in vectors))


def by_collectives(lengths, x, cot, matrices, vectors):
    gather = lambda a: lax.all_gather(a, "dp", axis=0, tiled=True)
    scatter = lambda a: lax.psum_scatter(a, "dp", scatter_dimension=0, tiled=True)
    results = whole(lengths, x, cot, [gather(m) for m in matrices], [gather(v) for v in vectors])
    return results[:2], [scatter(m) for m in results[2:6]], [scatter(v[0]) for v in results[6:]]


def by_kernel(lengths, x, cot, matrices, vectors, n):
    used = sum(v.shape[0] for v in vectors)
    row = jnp.concatenate(vectors + (jnp.zeros((128 - used,), BF16),)).astype(F32).reshape(1, 128)
    results = quick(lengths, x, cot, *matrices, row, n)
    pieces, at = [], 0
    for v in vectors:
        pieces.append(results[6][0, at : at + v.shape[0]])
        at += v.shape[0]
    return results[:2], results[2:6], pieces


def in_tiles(n, back_w, heads_w, up_w, down_w):
    rows = 2 * QUAD * down_w.shape[0]
    return (
        n % (2 * QUAD) == 0 and heads_w.shape[0] == 8 and up_w.shape[0] == 8
        and back_w.shape[0] % 16 == 0 and down_w.shape[0] % 16 == 0 and FF_STEP % rows == 0
    )


def local(n, block_in, lengths, back_w, back_b, heads_w, heads_b, norm1_gain, norm1_bias, norm2_gain, norm2_bias,
          up_w, up_b, down_w, down_b, cotangent):
    matrices = (back_w, heads_w, up_w, down_w)
    vectors = (back_b, heads_b, norm1_gain, norm1_bias, norm2_gain, norm2_bias, up_b, down_b)
    if in_tiles(n, *matrices):
        big, weights, small = by_kernel(lengths, block_in, cotangent, matrices, vectors, n)
    else:
        big, weights, small = by_collectives(lengths, block_in, cotangent, matrices, vectors)
    gback, gheads, gup, gdown = weights
    gb, gh, gg1, gb1, gg2, gb2, gu, gd = small
    return *big, gback, gb, gheads, gh, gg1, gb1, gg2, gb2, gup, gu, gdown, gd


def solution(mesh):
    n = mesh.shape["dp"]
    m, v = P("dp", None), P("dp")
    return jax.shard_map(
        functools.partial(local, n), mesh=mesh,
        in_specs=(m, v, m, v, m, v, v, v, v, v, m, v, m, v, m),
        out_specs=(m, m, m, v, m, v, v, v, v, v, m, v, m, v), check_vma=False,
    )
```

time: 1160 us -> 77.4 us (0.07)
  waiting for transfers between devices: 436 us -> 0 us
  other arithmetic: 262 us -> 0.52 us
  blocking collectives: 236 us -> 0 us
  local copies, waits for them, and re-layouts: 165 us -> 9.38 us
  Pallas kernels: 0 us -> 66.3 us
  matrix products: 40.7 us -> 0 us
  between operations: 14.5 us -> 0.75 us
    reduce_scatter x4 -> x0, waiting for transfers between devices: 436 us -> none  [the longest x1 137 us: local(): lax.psum_scatter(mlp_grads[2], 'dp', scatter_dimension=0, tiled=True)]
    all_gather x4 -> x0, blocking collectives: 157 us -> none  [the longest x1 41.4 us: local(): lax.all_gather(cell_set[0], 'dp', axis=0, tiled=True)]
    dot_general x32 -> x0, other arithmetic: 124 us -> none  [block_scan(): jnp.einsum('enfp,efp->enp', weight_tree, forcing_term)]
    squeeze x80 -> x3, local copies, waits for them, and re-layouts: 91.5 us -> 1.76 us  [by_kernel(): pieces.append(results[6][0, at:at + v.shape[0]])]
    unnamed x2 -> x0, blocking collectives: 79.3 us -> none
    reduce_sum x25 -> x0, other arithmetic: 78.4 us -> none  [the longest x16 65.4 us: block_scan(): summed_logarithm[:, :, None, :] - summed_logarithm[:, None, :, :]]
    pallas_call x0 -> x1, Pallas kernels: none -> 66.3 us  [quick(): pl.pallas_call(functools.partial(mega, INPUTS + OUTPUTS + tuple(space), (...]
    dot_general x15 -> x0, matrix products: 40.7 us -> none  [the longest x5 16.3 us: outer_sum(): lax.dot_general(left, right, (((0,), (0,)), ((), ())), preferred_element_...]
  transfers between devices with their start and end apart: 4 -> 0, of which waited for: 4 -> 0; matrix products, arithmetic and copies ran while one was open for 2% -> 0% of each run, Pallas kernels for 0% -> 0%
where the time goes in v1:
time: 77.4 us; the launch traced here: 77 us
  Pallas kernels  66.3 us (86%)
  local copies, waits for them, and re-layouts  9.38 us (12%)
    pallas_call x1, Pallas kernels, quick(): pl.pallas_call(functools.partial(mega, INPUTS + OUTPUTS + tuple(space), (...  66.3 us
    unnamed x34, local copies, waits for them, and re-layouts  7.51 us
    squeeze x3, local copies, waits for them, and re-layouts, by_kernel(): pieces.append(results[6][0, at:at + v.shape[0]])  1.76 us

profile of v1, /device:TPU:0, one launch (start us, length us, event | category | flops | bytes accessed | tf_op | source)
XLA Modules:
  0.0 77.0 jit_solution(18148307467177242674)
XLA Ops:
  0.6 0.0 copy-start.13
  0.7 0.0 copy-start.9
  0.7 0.0 copy-start.10
  0.7 0.0 copy-start.11
  0.7 0.0 copy-start.12
  0.7 0.0 copy-start.6
  0.7 0.0 copy-start.7
  0.7 0.0 copy-start.8
  0.7 0.6 copy-done.13
  1.3 0.0 copy-done.9
  1.3 0.0 copy-done.10
  1.3 0.0 copy-done.11
  1.4 0.0 copy-done.12
  1.4 0.0 copy-done.6
  1.4 0.0 copy-done.7
  1.4 0.0 copy-done.8
  1.4 0.1 concatenate.37
  1.5 0.5 convert_element_type.10.refs_7_
  2.0 66.3 %shard_map.254 = (bf16[2048,256]{1,0:T(8,128)(2,1)}, bf16[2048,256]{1,0:T(8,128)(2,1)}, f32[16,256]{1,0:T(8,128)}, f32[8,768]{1,0:T(8,128)}, f32[8,1024]{1,0:T(8...) custom-call(s32[2]{0:T(128)} %refs_0_.1, bf16[2048,256]{1,0:T(8,128)(2,1)} %refs_1_.1, bf16[2048,256]{1,0:T(8,128)(2,1)} %refs_2_.1, ...), custom_call_target="tpu_custom_call" | custom-call | tf_op jit(solution)/shard_map/pallas_call | solution.py:655
  68.4 0.0 copy-start.4
  68.4 0.6 copy-done.4
  69.0 0.6 slice_bitcast_fusion
  69.6 0.6 slice_bitcast_fusion.6
  70.2 0.6 slice_bitcast_fusion.1
  70.7 0.0 copy-start
  70.7 2.4 %copy.35 = bf16[2048,256]{1,0:T(8,128)(2,1)} copy(bf16[2048,256]{1,0:T(8,128)(2,1)} %get-tuple-element.48) | data formatting | bytes 2097152
  73.1 0.0 copy-done
  73.1 0.0 copy-start.5
  73.1 1.0 %copy.36 = bf16[2048,256]{1,0:T(8,128)(2,1)} copy(bf16[2048,256]{1,0:T(8,128)(2,1)S(1)} %copy-done) | data formatting | bytes 2097152
  74.1 0.0 copy-done.5
  74.1 0.0 copy-start.3
  74.1 0.6 copy.37
  74.7 0.1 copy-done.3
  74.8 0.0 copy-start.2
  74.8 0.6 copy.38
  75.4 0.2 copy-done.2
  75.6 0.0 copy-start.1
  75.6 0.6 copy.39
  76.2 0.2 copy-done.1
  76.4 0.6 copy.40
  (1 shorter events, 0.0 us)
Async XLA Ops:
  0.6 0.7 copy-start.13
  0.7 0.7 copy-start.9
  0.7 0.7 copy-start.10
  0.7 0.7 copy-start.11
  0.7 0.7 copy-start.12
  0.7 0.7 copy-start.6
  0.7 0.7 copy-start.7
  0.7 0.7 copy-start.8
  68.4 0.6 copy-start.4
  70.7 2.4 %copy-start = (bf16[2048,256]{1,0:T(8,128)(2,1)S(1)}, bf16[2048,256]{1,0:T(8,128)(2,1)}, u32[]{:S(2)}) copy-start(bf16[2048,256]{1,0:T(8,128)(2,1)} %get-tuple-element.49) | copy-start | bytes 3145732
  73.1 1.0 %copy-start.5 = (f32[16,256]{1,0:T(8,128)S(1)}, f32[16,256]{1,0:T(8,128)}, u32[]{:S(2)}) copy-start(f32[16,256]{1,0:T(8,128)} %get-tuple-element.50) | copy-start | bytes 49156
  74.1 0.7 copy-start.3
  74.8 0.8 copy-start.2
  75.6 0.8 %copy-start.1 = (f32[32,256]{1,0:T(8,128)S(1)}, f32[32,256]{1,0:T(8,128)}, u32[]{:S(2)}) copy-start(f32[32,256]{1,0:T(8,128)} %get-tuple-element.60) | copy-start | bytes 98308

commit v2 on v1

--- a/solution.py
+++ b/solution.py
@@ -59,15 +59,22 @@
     S, L, D = dims
     order = shuffle()
     sub = sublane((8, D))
-    joined = []
+    joined, cots = [], []
     for s in range(S):
+        cots.append(mm(order, r.cot[pl.ds(s * L + i * BLK, BLK), :]))
         mixed = mm(order, r.x[pl.ds(s * L + i * BLK, BLK), :])
         turned = pltpu.roll(mixed[BLK - 8 :], 1, 0)
         first = jnp.where(sub == 0, jnp.where(i == 0, 0.0, r.xcarry[s]), turned)
         r.xcarry[s] = turned
         before = jnp.concatenate([first, mixed[: BLK - 8]], axis=0)
         joined.append(jnp.concatenate([mixed, before], axis=1))
-    r.joined[block_rows(i, dims), :] = jnp.concatenate(joined, axis=0).astype(BF16)
+    rows = block_rows(i, dims)
+    r.joined[rows, :] = jnp.concatenate(joined, axis=0).astype(BF16)
+    cot = jnp.concatenate(cots, axis=0)
+    r.mixed_cot[rows, :] = cot.astype(BF16)
+    gout = jnp.where(live(i, r, dims), cot, 0.0)
+    r.gbd[...] += fold(gout)
+    r.gout[rows, :] = gout.astype(BF16)
 
 
 def backbone(i, r, dims):
@@ -140,7 +147,6 @@
     S, L, D = dims
     FF = r.wu.shape[1]
     rows = block_rows(i, dims)
-    order, back = shuffle(), shuffle(True)
     valid = live(i, r, dims)
     g1, b1, g2, b2 = r.g1[...], r.b1[...], r.g2[...], r.b2[...]
     xhat1, rs1 = normalise(r.state[rows, :], D)
@@ -148,13 +154,10 @@
     xhat2, rs2 = normalise(mid, D)
     normed = (xhat2 * g2 + b2).astype(BF16)
     r.normed[rows, :] = normed
-    cot = jnp.concatenate([mm(order, r.cot[pl.ds(s * L + i * BLK, BLK), :]) for s in range(S)], axis=0)
-    gout32 = jnp.where(valid, cot, 0.0)
-    r.gbd[...] += fold(gout32)
-    gout = gout32.astype(BF16)
-    r.gout[rows, :] = gout
+    r.mid[rows, :] = mid
+    gout = r.gout[rows, :]
     W = FF_STEP
-    y = gn = None
+    gn = None
     for n in range(FF // W):
         cols = slice(n * W, (n + 1) * W)
         down = r.wd_rows(n, W)
@@ -162,22 +165,16 @@
         v2 = pu * pu
         h = 0.5 * jnp.tanh(pu * (v2 * (GC * GA) + GC)) + 0.5
         hid = pu * h
-        hid16 = hid.astype(BF16)
-        r.hidden[rows, cols] = hid16
+        r.hidden[rows, cols] = hid.astype(BF16)
         slope = h + hid * (1.0 - h) * (v2 * (6.0 * GA * GC) + 2.0 * GC)
         gpu = (mm_nt(gout, down) * slope).astype(BF16)
         r.gpu[rows, cols] = gpu
         r.gbu[:, cols] += fold(gpu.astype(F32))
-        yn = mm(hid16, down)
         gnn = mm_nt(gpu, r.wu[:, cols])
-        y = yn if y is None else y + yn
         gn = gnn if gn is None else gn + gnn
-    out = (mid + jnp.where(valid, y + r.bd[...], 0.0)).astype(BF16)
-    for s in range(S):
-        r.out[pl.ds(s * L + i * BLK, BLK), :] = mm(back, out[s * BLK : (s + 1) * BLK]).astype(BF16)
     r.gg2[...] += fold(gn * xhat2)
     r.gb2[...] += fold(gn)
-    gmid = cot + norm_back(gn, g2, xhat2, rs2, D)
+    gmid = r.mixed_cot[rows, :].astype(F32) + norm_back(gn, g2, xhat2, rs2, D)
     r.gmid[rows, :] = gmid
     dy1 = jnp.where(valid, gmid, 0.0)
     r.gg1[...] += fold(dy1 * xhat1)
@@ -237,6 +234,16 @@
     r.gbb[...] += fold(gpb.astype(F32))
 
 
+def emit(i, r, dims):
+    S, L, D = dims
+    rows = block_rows(i, dims)
+    back = shuffle(True)
+    branch = mm(r.hidden[rows, :], flat(r.wd)) + r.bd[...]
+    out = (r.mid[rows, :] + jnp.where(live(i, r, dims), branch, 0.0)).astype(BF16)
+    for s in range(S):
+        r.out[pl.ds(s * L + i * BLK, BLK), :] = mm(back, out[s * BLK : (s + 1) * BLK]).astype(BF16)
+
+
 def leave(i, r, dims):
     S, L, D = dims
     nb = L // BLK
@@ -277,7 +284,7 @@
         o=v((T, D), F32), v=v((T, D), F32), f=v((T, D), F32), state=v((T, D), F32),
         start=v((L // BLK, S, 8, D), F32), xcarry=v((S, 8, D), F32), scarry=v((S, 8, D), F32),
         normed=v((T, D), BF16), gout=v((T, D), BF16), hidden=v((T, FF), BF16), gpu=v((T, FF), BF16),
-        gmid=v((T, D), F32), gnorm=v((T, D), F32), gph=v((T, 3 * D), BF16), gpb=v((T, D), BF16),
+        mixed_cot=v((T, D), BF16), mid=v((T, D), F32), gmid=v((T, D), F32), gnorm=v((T, D), F32), gph=v((T, 3 * D), BF16), gpb=v((T, D), BF16),
     )
     for name, width in zip(SUMS, sum_widths(D, FF)):
         space[name] = v((8, width), F32)
@@ -319,8 +326,10 @@
     def device(self, z, q):
         return (z * QUAD + q) * 2 + self.c
 
-    def others(self):
-        return [(a, b) for a in range(self.planes) for b in range(QUAD) if a or b]
+    def peers(self):
+        found = [self.device(self.plane(a), self.q) for a in range(1, self.planes)]
+        found += [self.device(self.z, self.corner(b)) for b in range(1, QUAD)]
+        return found + [self.partner]
 
 
 class Copies:
@@ -362,8 +371,8 @@
 
 
 class Share:
-    def __init__(self, r, name, cutter, copies, place, direct):
-        self.r, self.name, self.cut, self.copies, self.p, self.direct = r, name, cutter, copies, place, direct
+    def __init__(self, r, name, cutter, copies, place):
+        self.r, self.name, self.cut, self.copies, self.p = r, name, cutter, copies, place
 
     def ref(self, kind):
         return getattr(self.r, kind + self.name)
@@ -371,68 +380,52 @@
     def pair(self):
         p = self.p
         self.ref("cs")[...] = self.cut(self.ref("dw")[:, :, 1 - p.c]).astype(BF16)
-        self.paired = self.copies.start(self.ref("cs"), self.ref("cr"), p.partner)
+        self.sent = [self.copies.start(self.ref("cs"), self.ref("cr"), p.partner)]
 
     def spread(self):
         p = self.p
-        self.paired.wait_recv()
+        arrived(self.sent)
         total = self.cut(self.ref("dw")[:, :, p.c]) + self.ref("cr")[...].astype(F32)
-        xs = self.ref("xs")
-        xs[...] = total.astype(BF16)
+        self.ref("xs")[...] = total.astype(BF16)
         self.sent = []
-        if self.direct:
-            for k, (a, b) in enumerate(p.others()):
-                z, q = p.plane(a), p.corner(b)
-                self.sent.append(self.copies.start(xs.at[z, q], self.ref("xr").at[k], p.device(z, q)))
-        else:
-            for b in range(1, QUAD):
-                q = p.corner(b)
-                self.sent.append(self.copies.start(xs.at[:, q], self.ref("xr").at[b - 1], p.device(p.z, q)))
+        for b in range(1, QUAD):
+            q = p.corner(b)
+            self.sent.append(self.copies.start(self.ref("xs").at[:, q], self.ref("xr").at[b - 1], p.device(p.z, q)))
 
     def climb(self):
         p = self.p
         arrived(self.sent)
-        acc = self.cut(self.ref("dw")[:, p.q, p.c]) + self.ref("cr")[:, p.q].astype(F32)
+        total = self.cut(self.ref("dw")[:, p.q, p.c]) + self.ref("cr")[:, p.q].astype(F32)
         for b in range(QUAD - 1):
-            acc = acc + self.ref("xr")[b].astype(F32)
-        self.ref("ac")[...] = acc
-        self.ref("zs")[...] = acc.astype(BF16)
+            total = total + self.ref("xr")[b].astype(F32)
+        self.ref("ac")[...] = total
+        self.ref("zs")[...] = total.astype(BF16)
         self.sent = []
         for a in range(1, p.planes):
             z = p.plane(a)
             self.sent.append(self.copies.start(self.ref("zs").at[z], self.ref("zr").at[a - 1], p.device(z, p.q)))
 
     def land(self):
-        p = self.p
         arrived(self.sent)
-        if self.direct:
-            acc = self.cut(self.ref("dw")[p.z, p.q, p.c]) + self.ref("cr")[p.z, p.q].astype(F32)
-            for k in range(len(self.sent)):
-                acc = acc + self.ref("xr")[k].astype(F32)
-        else:
-            acc = self.ref("ac")[p.z]
-            for k in range(len(self.sent)):
-                acc = acc + self.ref("zr")[k].astype(F32)
-        return acc
-
-
-def share_space(name, n, rows, columns, cutting, direct):
+        total = self.ref("ac")[self.p.z]
+        for k in range(self.p.planes - 1):
+            total = total + self.ref("zr")[k].astype(F32)
+        return total
+
+
+def share_space(name, n, rows, columns, cutting):
     Z, v = n // (2 * QUAD), pltpu.VMEM
     R, C = (2 * rows, columns // 2) if cutting else (rows, columns)
-    space = {
+    return {
         "dw" + name: v((Z, QUAD, 2, rows, columns), F32),
         "cs" + name: v((Z, QUAD, R, C), BF16),
         "cr" + name: v((Z, QUAD, R, C), BF16),
         "xs" + name: v((Z, QUAD, R, C), BF16),
+        "xr" + name: v((QUAD - 1, Z, R, C), BF16),
+        "ac" + name: v((Z, R, C), F32),
+        "zs" + name: v((Z, R, C), BF16),
+        "zr" + name: v((Z - 1, R, C), BF16),
     }
-    if direct:
-        space["xr" + name] = v((Z * QUAD - 1, R, C), BF16)
-    else:
-        space["xr" + name] = v((QUAD - 1, Z, R, C), BF16)
-        space["ac" + name] = v((Z, R, C), F32)
-        space["zs" + name] = v((Z, R, C), BF16)
-        space["zr" + name] = v((Z - 1, R, C), BF16)
-    return space
 
 
 def segments(n, D, FF):
@@ -452,11 +445,12 @@
 
 
 def owners(n, D, FF):
-    parts = []
+    parts, Z = [], n // (2 * QUAD)
     for name, lane, width, own, offset in segments(n, D, FF):
         l = lax.broadcasted_iota(jnp.int32, (n, width), 1).astype(F32)
         row = lax.broadcasted_iota(jnp.int32, (n, width), 0)
-        device = (2 * (row % (n // 2)) + row // (n // 2)).astype(F32)
+        z, q, c = row % Z, row // Z % QUAD, row // (Z * QUAD)
+        device = ((z * QUAD + q) * 2 + c).astype(F32)
         parts.append(jnp.floor((l + 0.5) * (1.0 / own)) == device)
     return jnp.concatenate(parts, axis=1)
 
@@ -471,8 +465,6 @@
     S, L, D = dims
     nb = L // BLK
     p = Place(n)
-    chips = n // 2
-    chip = p.z * QUAD + p.q
     copies = Copies(r.send, r.recv)
 
     def run(f, first, last, down=False):
@@ -482,14 +474,13 @@
         lax.fori_loop(first, last, step, 0)
 
     barrier = pltpu.get_barrier_semaphore()
-    for a, b in p.others():
-        pl.semaphore_signal(barrier, inc=1, device_id=(p.device(p.plane(a), p.corner(b)),), device_id_type=MESH)
-    pl.semaphore_signal(barrier, inc=1, device_id=(p.partner,), device_id_type=MESH)
+    for peer in p.peers():
+        pl.semaphore_signal(barrier, inc=1, device_id=(peer,), device_id_type=MESH)
 
     loads = [
         pltpu.make_async_copy(src, dst, r.local.at[k])
         for k, (src, dst) in enumerate((
-            (r.wb_own, r.wb.at[p.z, p.q, p.c]), (r.vec_own, r.vec.at[p.c, pl.ds(chip, 1)]),
+            (r.wb_own, r.wb.at[p.z, p.q, p.c]), (r.vec_own, r.vec.at[p.c, p.q, pl.ds(p.z, 1)]),
             (r.wh_own, r.wh_mine), (r.wu_own, r.wu_mine), (r.wd_own, r.wd.at[p.z, p.q, p.c]),
             (r.x_hbm, r.x), (r.cot_hbm, r.cot),
         ))
@@ -500,47 +491,41 @@
         load.wait()
     r.wh_cut[p.z, p.q, p.c] = cut(r.wh_mine[...].astype(F32)).astype(BF16)
     r.wu_cut[p.z, p.q, p.c] = cut(r.wu_mine[...].astype(F32)).astype(BF16)
-    pl.semaphore_wait(barrier, len(p.others()) + 1)
-
-    def send_all(ref):
-        return [
-            copies.start(ref.at[p.z, p.q, p.c], ref.at[p.z, p.q, p.c], p.device(p.plane(a), p.corner(b)))
-            for a, b in p.others()
-        ]
-
-    def send_planes(ref):
-        return [
-            copies.start(ref.at[p.z, p.q, p.c], ref.at[p.z, p.q, p.c], p.device(p.plane(a), p.q))
-            for a in range(1, p.planes)
-        ]
-
-    def send_corners(ref):
-        return [
-            copies.start(ref.at[:, p.q, p.c], ref.at[:, p.q, p.c], p.device(p.z, p.corner(b)))
-            for b in range(1, QUAD)
-        ]
-
-    def send_pair(ref):
-        return [copies.start(ref.at[:, :, p.c], ref.at[:, :, p.c], p.partner)]
-
-    wb_in = send_all(r.wb)
-    vec_in = [
-        copies.start(r.vec.at[p.c, pl.ds(chip, 1)], r.vec.at[p.c, pl.ds(chip, 1)], p.device(p.plane(a), p.corner(b)))
-        for a, b in p.others()
-    ]
-    wh_in = send_all(r.wh_cut)
-    up_in = send_planes(r.wu_cut)
-    down_in = send_planes(r.wd)
+    pl.semaphore_wait(barrier, len(p.peers()))
+
+    def to_planes(own):
+        return [copies.start(own, own, p.device(p.plane(a), p.q)) for a in range(1, p.planes)]
+
+    def to_corners(own):
+        return [copies.start(own, own, p.device(p.z, p.corner(b))) for b in range(1, QUAD)]
+
+    def to_partner(own):
+        return [copies.start(own, own, p.partner)]
+
+    weights = (r.wb, r.wh_cut, r.wu_cut, r.wd)
+    wb_in = to_planes(r.wb.at[p.z, p.q, p.c])
+    vec_in = to_planes(r.vec.at[p.c, p.q, pl.ds(p.z, 1)])
+    wh_in, up_in, down_in = (to_planes(ref.at[p.z, p.q, p.c]) for ref in weights[1:])
 
     zero_sums(r)
+    arrived(wb_in)
+    wb_in = to_corners(r.wb.at[:, p.q, p.c])
+    arrived(vec_in)
+    vec_in = to_corners(r.vec.at[p.c, p.q])
+    arrived(wh_in)
+    wh_in = to_corners(r.wh_cut.at[:, p.q, p.c])
+    loads[5].wait()
+    loads[6].wait()
+    run(enter, 0, nb)
     fill_pick(r, n, D, FF)
-    loads[5].wait()
-    run(enter, 0, nb)
-
     arrived(wb_in)
-    wb_in = send_pair(r.wb)
+    wb_in = to_partner(r.wb.at[:, :, p.c])
     arrived(vec_in)
-    vec_in = [copies.start(r.vec.at[p.c], r.vec.at[p.c], p.partner)]
+    vec_in = to_partner(r.vec.at[p.c])
+    arrived(up_in)
+    up_in = to_corners(r.wu_cut.at[:, p.q, p.c])
+    arrived(down_in)
+    down_in = to_corners(r.wd.at[:, p.q, p.c])
     arrived(wb_in)
     arrived(vec_in)
     spread = mm_nt(r.vec[...].reshape(n, 128).astype(BF16), r.pick[...])
@@ -548,32 +533,25 @@
     for name, lane, width, own, offset in segments(n, D, FF):
         getattr(r, name)[...] = vectors[:, lane : lane + width]
 
+    arrived(wh_in)
+    wh_in = to_partner(r.wh_cut.at[:, :, p.c])
     run(backbone, 0, nb)
-    arrived(wh_in)
-    wh_in = send_pair(r.wh_cut)
-    arrived(up_in)
-    up_in = send_corners(r.wu_cut)
-    arrived(down_in)
-    down_in = send_corners(r.wd)
     arrived(wh_in)
     r.wh[...] = uncut(r.wh_cut[...].astype(F32)).reshape(D, 3 * D).astype(BF16)
     run(gates, 0, nb)
     arrived(up_in)
-    up_in = send_pair(r.wu_cut)
+    up_in = to_partner(r.wu_cut.at[:, :, p.c])
     arrived(down_in)
-    down_in = send_pair(r.wd)
+    down_in = to_partner(r.wd.at[:, :, p.c])
     arrived(up_in)
     r.wu[...] = uncut(r.wu_cut[...].astype(F32)).reshape(D, FF).astype(BF16)
     arrived(down_in)
-    loads[6].wait()
     run(feed_forward, 0, nb)
-    outs = [pltpu.make_async_copy(r.out, r.out_hbm, r.local.at[7])]
-    outs[0].start()
-
-    up = Share(r, "u", cut, copies, p, False)
-    down = Share(r, "d", same, copies, p, False)
-    heads = Share(r, "h", cut, copies, p, True)
-    back = Share(r, "b", same, copies, p, True)
+
+    up = Share(r, "u", cut, copies, p)
+    down = Share(r, "d", same, copies, p)
+    heads = Share(r, "h", cut, copies, p)
+    back = Share(r, "b", same, copies, p)
     r.dwu[...] = mm_tn(r.normed[...], r.gpu[...]).reshape(r.dwu.shape)
     up.pair()
     r.dwd[...] = mm_tn(r.gout[...], r.hidden[...]).T.reshape(r.dwd.shape)
@@ -581,44 +559,54 @@
     run(gates_back, 0, 1, True)
     up.spread()
     down.spread()
-    run(gates_back, 1, nb - 1, True)
-    up.climb()
-    down.climb()
-    run(gates_back, nb - 1, nb, True)
+    run(gates_back, 1, nb, True)
     r.dwh[...] = mm_tn(r.feat[...], r.gph[...]).reshape(r.dwh.shape)
     heads.pair()
     r.dwb[...] = mm_tn(r.gpb[...], r.joined[...]).T.reshape(r.dwb.shape)
     back.pair()
 
     sums = jnp.concatenate([jnp.sum(getattr(r, name)[...], axis=0, keepdims=True) for name in SUMS], axis=1)
-    mine = owners(n, D, FF)
-    rest, rows = jnp.where(mine, sums, 0.0), None
+    rest, rows = jnp.where(owners(n, D, FF), sums, 0.0), None
     for _ in range(3):
         part = rest.astype(BF16)
         rest = rest - part.astype(F32)
         row = mm(part, r.pick[...])
         rows = row if rows is None else rows + row
-    r.vs[...] = rows.reshape(2, chips, 128)
-    vec_pair = copies.start(r.vs.at[1 - p.c], r.vr, p.partner)
-    run(leave, 0, 1, True)
+    r.vs[...] = rows.reshape(r.vs.shape)
+    vec_out = [copies.start(r.vs.at[1 - p.c], r.vr, p.partner)]
     heads.spread()
     back.spread()
-    vec_pair.wait_recv()
+    arrived(vec_out)
     r.va[...] = r.vs[p.c] + r.vr[...]
     vec_out = []
-    for a, b in p.others():
-        z, q = p.plane(a), p.corner(b)
-        vec_out.append(copies.start(r.va.at[pl.ds(z * QUAD + q, 1)], r.vt.at[pl.ds(chip, 1)], p.device(z, q)))
-    r.vt[pl.ds(chip, 1), :] = r.va[pl.ds(chip, 1), :]
-    run(leave, 1, nb, True)
-    outs.append(pltpu.make_async_copy(r.ig, r.ig_hbm, r.local.at[8]))
+    for b in range(1, QUAD):
+        q = p.corner(b)
+        vec_out.append(copies.start(r.va.at[q], r.vx.at[b - 1], p.device(p.z, q)))
+    up.climb()
+    down.climb()
+    run(leave, 0, nb, True)
+    outs = [pltpu.make_async_copy(r.ig, r.ig_hbm, r.local.at[7])]
+    outs[0].start()
+    heads.climb()
+    back.climb()
+    arrived(vec_out)
+    total = r.va[p.q]
+    for b in range(QUAD - 1):
+        total = total + r.vx[b]
+    r.vz[...] = total
+    vec_out = []
+    for a in range(1, p.planes):
+        z = p.plane(a)
+        vec_out.append(copies.start(r.vz.at[pl.ds(z, 1)], r.vt.at[pl.ds(a - 1, 1)], p.device(z, p.q)))
+    run(emit, 0, nb)
+    outs.append(pltpu.make_async_copy(r.out, r.out_hbm, r.local.at[8]))
     outs[1].start()
     r.gup[...] = uncut(up.land())
     r.gdown[...] = down.land()
     r.gheads[...] = uncut(heads.land())
     r.gback[...] = back.land()
     arrived(vec_out)
-    r.gvec[...] = jnp.sum(r.vt[...], axis=0, keepdims=True)
+    r.gvec[...] = r.vz[pl.ds(p.z, 1), :] + jnp.sum(r.vt[...], axis=0, keepdims=True)
     copies.finish()
     for out in outs:
         out.wait()
@@ -628,7 +616,7 @@
     S = lengths.shape[0]
     T, D = x.shape
     L, FF = T // S, wu.shape[1]
-    Z, chips, v = n // (2 * QUAD), n // 2, pltpu.VMEM
+    Z, v = n // (2 * QUAD), pltpu.VMEM
     space = work_space(S, L, D, FF)
     rb, rh, ru, rd = wb.shape[0], wh.shape[0], wu.shape[0], wd.shape[0]
     space.update(
@@ -636,30 +624,80 @@
         wb=v((Z, QUAD, 2, rb, D), BF16), wd=v((Z, QUAD, 2, rd, D), BF16),
         wh_cut=v((Z, QUAD, 2, 2 * rh, 3 * D // 2), BF16), wu_cut=v((Z, QUAD, 2, 2 * ru, FF // 2), BF16),
         wh=v((D, 3 * D), BF16), wu=v((D, FF), BF16), wh_mine=v((rh, 3 * D), BF16), wu_mine=v((ru, FF), BF16),
-        vec=v((2, chips, 128), F32), pick=v((sum(sum_widths(D, FF)), 128), BF16),
-        vs=v((2, chips, 128), F32), vr=v((chips, 128), F32), va=v((chips, 128), F32), vt=v((chips, 128), F32),
-        local=pltpu.SemaphoreType.DMA((9,)), send=pltpu.SemaphoreType.DMA((160,)), recv=pltpu.SemaphoreType.DMA((160,)),
+        vec=v((2, QUAD, Z, 128), F32), pick=v((sum(sum_widths(D, FF)), 128), BF16),
+        vs=v((2, QUAD, Z, 128), F32), vr=v((QUAD, Z, 128), F32), va=v((QUAD, Z, 128), F32),
+        vx=v((QUAD - 1, Z, 128), F32), vz=v((Z, 128), F32), vt=v((Z - 1, 128), F32),
+        local=pltpu.SemaphoreType.DMA((9,)), send=pltpu.SemaphoreType.DMA((72,)), recv=pltpu.SemaphoreType.DMA((72,)),
     )
     for name, lane, width, own, offset in segments(n, D, FF):
         space[name] = v((1, width), F32)
-    space.update(share_space("u", n, ru, FF, True, False))
-    space.update(share_space("d", n, rd, D, False, False))
-    space.update(share_space("h", n, rh, 3 * D, True, True))
-    space.update(share_space("b", n, rb, D, False, True))
+    space.update(share_space("u", n, ru, FF, True))
+    space.update(share_space("d", n, rd, D, False))
+    space.update(share_space("h", n, rh, 3 * D, True))
+    space.update(share_space("b", n, rb, D, False))
     row = lambda a, b: jax.ShapeDtypeStruct((a, b), F32)
     shapes = (
         jax.ShapeDtypeStruct((T, D), BF16), jax.ShapeDtypeStruct((T, D), BF16),
         row(rb, D), row(rh, 3 * D), row(ru, FF), row(rd, D), row(1, 128),
     )
     hbm, vmem = pl.BlockSpec(memory_space=pl.ANY), pl.BlockSpec(memory_space=pltpu.VMEM)
-    return pl.pallas_call(
+    results = pl.pallas_call(
         functools.partial(mega, INPUTS + OUTPUTS + tuple(space), (S, L, D), n, FF),
         out_shape=shapes,
         in_specs=[pl.BlockSpec(memory_space=pltpu.SMEM)] + [hbm] * 7,
-        out_specs=[hbm, hbm] + [vmem] * 5,
+        out_specs=[hbm] * 2 + [vmem] * 5,
         scratch_shapes=list(space.values()),
         compiler_params=pltpu.CompilerParams(collective_id=0, has_side_effects=True, vmem_limit_bytes=62 << 20),
     )(lengths, x, cot, wb, wh, wu, wd, vectors)
+    return hand_over(results, [own for name, lane, width, own, offset in segments(n, D, FF)])
+
+
+def hand_over_kernel(widths, parts, *refs):
+    count = len(parts)
+    sources, targets = refs[: count + 1], refs[count + 1 : 2 * count + 1]
+    smalls = refs[2 * count + 1 : 2 * count + 1 + len(widths)]
+    stages, sem_in, sem_out = refs[-count - 3 : -2], refs[-2], refs[-1]
+    moves, k = [], 0
+    for source, stage, cuts in zip(sources, stages, (1,) + parts):
+        rows = source.shape[0] // cuts
+        for j in range(cuts):
+            piece = pl.ds(j * rows, rows)
+            move = pltpu.make_async_copy(source.at[piece], stage.at[piece], sem_in.at[k])
+            move.start()
+            moves.append((move, stage.at[piece], piece))
+            k += 1
+    moves[0][0].wait()
+    at = 0
+    for small, width in zip(smalls, widths):
+        small[...] = pltpu.roll(stages[0][...], (128 - at) % 128, 1)[:, :width]
+        at += width
+    k, out = 1, []
+    for target, cuts in zip(targets, parts):
+        for j in range(cuts):
+            move, stage, piece = moves[k]
+            move.wait()
+            out.append(pltpu.make_async_copy(stage, target.at[piece], sem_out.at[k - 1]))
+            out[-1].start()
+            k += 1
+    for move in out:
+        move.wait()
+
+
+def hand_over(results, widths):
+    hbm, vmem = pl.BlockSpec(memory_space=pl.ANY), pl.BlockSpec(memory_space=pltpu.VMEM)
+    results = results[6:] + results[:6]
+    parts = (4, 4, 1, 1, 1, 1)
+    shapes = [jax.ShapeDtypeStruct(a.shape, a.dtype) for a in results[1:]]
+    shapes += [jax.ShapeDtypeStruct((1, w), F32) for w in widths]
+    return pl.pallas_call(
+        functools.partial(hand_over_kernel, widths, parts),
+        out_shape=shapes,
+        in_specs=[hbm] * len(results),
+        out_specs=[hbm] * len(parts) + [vmem] * len(widths),
+        scratch_shapes=[pltpu.VMEM(a.shape, a.dtype) for a in results]
+        + [pltpu.SemaphoreType.DMA((sum(parts) + 1,)), pltpu.SemaphoreType.DMA((sum(parts),))],
+        compiler_params=pltpu.CompilerParams(vmem_limit_bytes=62 << 20),
+    )(*results)
 
 
 def plain(names, dims, *refs):
@@ -678,6 +716,7 @@
         run(f)
     r.gup[...] = mm_tn(r.normed[...], r.gpu[...])
     r.gdown[...] = mm_tn(r.gout[...], r.hidden[...]).T
+    run(emit)
     run(gates_back, True)
     r.gheads[...] = mm_tn(r.feat[...], r.gph[...])
     r.gback[...] = mm_tn(r.gpb[...], r.joined[...]).T
@@ -718,11 +757,7 @@
     used = sum(v.shape[0] for v in vectors)
     row = jnp.concatenate(vectors + (jnp.zeros((128 - used,), BF16),)).astype(F32).reshape(1, 128)
     results = quick(lengths, x, cot, *matrices, row, n)
-    pieces, at = [], 0
-    for v in vectors:
-        pieces.append(results[6][0, at : at + v.shape[0]])
-        at += v.shape[0]
-    return results[:2], results[2:6], pieces
+    return results[:2], results[2:6], [row[0] for row in results[6:]]
 
 
 def in_tiles(n, back_w, heads_w, up_w, down_w):

time: 77.4 us -> 58.2 us (0.75)
  Pallas kernels: 66.3 us -> 55.9 us
  local copies, waits for them, and re-layouts: 9.38 us -> 0.79 us
    pallas_call x1, Pallas kernels: 66.3 us -> 52.9 us  [quick(): pl.pallas_call(functools.partial(mega, INPUTS + OUTPUTS + tuple(space), (...]
    unnamed x34 -> x16, local copies, waits for them, and re-layouts: 7.51 us -> 0.69 us
    pallas_call x0 -> x1, Pallas kernels: none -> 3.05 us  [hand_over(): pl.pallas_call(functools.partial(hand_over_kernel, widths, parts), out_sh...]
    squeeze x3 -> x0, local copies, waits for them, and re-layouts: 1.76 us -> none  [by_kernel(): pieces.append(results[6][0, at:at + v.shape[0]])]
where the time goes in v2:
time: 58.2 us; the launch traced here: 58 us
  Pallas kernels  55.9 us (96%)
  local copies, waits for them, and re-layouts  0.79 us (1%)
  between operations  0.73 us (1%)
    pallas_call x1, Pallas kernels, quick(): pl.pallas_call(functools.partial(mega, INPUTS + OUTPUTS + tuple(space), (...  52.9 us
    pallas_call x1, Pallas kernels, hand_over(): pl.pallas_call(functools.partial(hand_over_kernel, widths, parts), out_sh...  3.05 us

profile of v2, /device:TPU:0, one launch (start us, length us, event | category | flops | bytes accessed | tf_op | source)
XLA Modules:
  0.0 58.0 jit_solution(4117442762221816494)
XLA Ops:
  0.6 0.0 copy-start.7
  0.7 0.0 copy-start.3
  0.7 0.0 copy-start.4
  0.7 0.0 copy-start.5
  0.7 0.0 copy-start.6
  0.7 0.0 copy-start
  0.7 0.0 copy-start.1
  0.7 0.0 copy-start.2
  0.7 0.6 copy-done.7
  1.3 0.0 copy-done.3
  1.3 0.0 copy-done.4
  1.3 0.0 copy-done.5
  1.4 0.0 copy-done.6
  1.4 0.0 copy-done
  1.4 0.0 copy-done.1
  1.4 0.0 copy-done.2
  1.4 0.1 concatenate.37
  1.5 0.5 convert_element_type.10.refs_7_
  2.0 52.9 %shard_map.254 = (bf16[2048,256]{1,0:T(8,128)(2,1)}, bf16[2048,256]{1,0:T(8,128)(2,1)}, f32[16,256]{1,0:T(8,128)}, f32[8,768]{1,0:T(8,128)}, f32[8,1024]{1,0:T(8...) custom-call(s32[2]{0:T(128)} %refs_0_.1, bf16[2048,256]{1,0:T(8,128)(2,1)} %refs_1_.1, bf16[2048,256]{1,0:T(8,128)(2,1)} %refs_2_.1, ...), custom_call_target="tpu_custom_call" | custom-call | tf_op jit(solution)/shard_map/pallas_call | solution.py:644
  54.9 3.1 %shard_map.255 = (bf16[2048,256]{1,0:T(8,128)(2,1)}, bf16[2048,256]{1,0:T(8,128)(2,1)}, f32[16,256]{1,0:T(8,128)}, f32[8,768]{1,0:T(8,128)}, f32[8,1024]{1,0:T(8...) custom-call(f32[1,128]{1,0:T(1,128)} %get-tuple-element.35.refs_0_, ...), custom_call_target="tpu_custom_call" | custom-call | tf_op jit(solution)/shard_map/pallas_call | solution.py:692
  (1 shorter events, 0.0 us)
Async XLA Ops:
  0.6 0.7 %copy-start.7 = (bf16[8]{0:T(256)(128)(2,1)S(1)}, bf16[8]{0:T(256)(128)(2,1)}, u32[]{:S(2)}) copy-start(bf16[8]{0:T(256)(128)(2,1)} %param.28) | copy-start | bytes 52
  0.7 0.7 %copy-start.3 = (bf16[8]{0:T(256)(128)(2,1)S(1)}, bf16[8]{0:T(256)(128)(2,1)}, u32[]{:S(2)}) copy-start(bf16[8]{0:T(256)(128)(2,1)} %param.22) | copy-start | bytes 52
  0.7 0.7 %copy-start.4 = (bf16[8]{0:T(256)(128)(2,1)S(1)}, bf16[8]{0:T(256)(128)(2,1)}, u32[]{:S(2)}) copy-start(bf16[8]{0:T(256)(128)(2,1)} %param.23) | copy-start | bytes 52
  0.7 0.7 %copy-start.5 = (bf16[8]{0:T(256)(128)(2,1)S(1)}, bf16[8]{0:T(256)(128)(2,1)}, u32[]{:S(2)}) copy-start(bf16[8]{0:T(256)(128)(2,1)} %param.24) | copy-start | bytes 52
  0.7 0.7 %copy-start.6 = (bf16[32]{0:T(256)(128)(2,1)S(1)}, bf16[32]{0:T(256)(128)(2,1)}, u32[]{:S(2)}) copy-start(bf16[32]{0:T(256)(128)(2,1)} %param.26) | copy-start | bytes 196
  0.7 0.7 %copy-start = (bf16[8]{0:T(256)(128)(2,1)S(1)}, bf16[8]{0:T(256)(128)(2,1)}, u32[]{:S(2)}) copy-start(bf16[8]{0:T(256)(128)(2,1)} %param.18) | copy-start | bytes 52
  0.7 0.7 %copy-start.1 = (bf16[24]{0:T(256)(128)(2,1)S(1)}, bf16[24]{0:T(256)(128)(2,1)}, u32[]{:S(2)}) copy-start(bf16[24]{0:T(256)(128)(2,1)} %param.20) | copy-start | bytes 148
  0.7 0.7 %copy-start.2 = (bf16[8]{0:T(256)(128)(2,1)S(1)}, bf16[8]{0:T(256)(128)(2,1)}, u32[]{:S(2)}) copy-start(bf16[8]{0:T(256)(128)(2,1)} %param.21) | copy-start | bytes 52

commit v3 on v2

--- a/solution.py
+++ b/solution.py
@@ -11,6 +11,7 @@
 STEPS = BLK // LANES
 QUAD = 4
 FF_STEP = 256
+UP_PLANE, DOWN_PLANE, HEADS_PLANE, BACK_PLANE = False, False, False, True
 F32 = jnp.float32
 BF16 = jnp.bfloat16
 MESH = pl.DeviceIdType.MESH
@@ -52,7 +53,18 @@
 
 
 def block_rows(i, dims):
-    return pl.ds(i * (dims[0] * BLK), dims[0] * BLK)
+    return pl.ds(pl.multiple_of(i * (dims[0] * BLK), dims[0] * BLK), dims[0] * BLK)
+
+
+def add_to(ref, columns, values):
+    ref[..., columns] += values.reshape(ref.shape[:-1] + values.shape[-1:])
+
+
+def live(i, r, dims):
+    S, L, D = dims
+    row = lax.broadcasted_iota(jnp.int32, (BLK, D), 0)
+    time = (row & 7) * STEPS + (row >> 3) + i * BLK
+    return jnp.concatenate([time < r.lengths[s] for s in range(S)], axis=0)
 
 
 def enter(i, r, dims):
@@ -69,19 +81,26 @@
         before = jnp.concatenate([first, mixed[: BLK - 8]], axis=0)
         joined.append(jnp.concatenate([mixed, before], axis=1))
     rows = block_rows(i, dims)
-    r.joined[rows, :] = jnp.concatenate(joined, axis=0).astype(BF16)
+    joined = jnp.concatenate(joined, axis=0).astype(BF16)
+    r.joined[rows, :] = joined
+    r.joined_t[pl.ds(0, 2 * D), rows] = joined.T
     cot = jnp.concatenate(cots, axis=0)
     r.mixed_cot[rows, :] = cot.astype(BF16)
     gout = jnp.where(live(i, r, dims), cot, 0.0)
     r.gbd[...] += fold(gout)
-    r.gout[rows, :] = gout.astype(BF16)
+    half = (0.5 * gout).astype(BF16)
+    r.half[rows, :] = half
+    r.half_t[:, rows] = half.T
 
 
 def backbone(i, r, dims):
+    S, L, D = dims
     rows = block_rows(i, dims)
     inner = jnp.tanh(0.666 * (mm(r.joined[rows, :], flat(r.wb)) + r.bb[...]))
-    r.inner[rows, :] = inner
-    r.feat[rows, :] = (1.7159 * inner).astype(BF16)
+    r.bend[rows, :] = (1.7159 * 0.666) * (1.0 - inner * inner)
+    feat = (1.7159 * inner).astype(BF16)
+    r.feat[rows, :] = feat
+    r.feat_t[pl.ds(0, D), rows] = feat.T
 
 
 def gates(i, r, dims):
@@ -92,11 +111,13 @@
     o = 0.5 * jnp.tanh(0.5 * heads[:, :D]) + 0.5
     v = jnp.tanh(heads[:, D : 2 * D])
     f = jnp.tanh(heads[:, 2 * D :])
-    r.o[rows, :] = o
-    r.v[rows, :] = v
-    r.f[rows, :] = f
     keep = 1.0 - o
-    drive = f + o * (v - f)
+    gap = v - f
+    drive = f + o * gap
+    r.keep[rows, :] = keep
+    r.to_value[rows, :] = o * (1.0 - v * v)
+    r.to_fallback[rows, :] = keep * (1.0 - f * f)
+    bend = o * keep
     one = jnp.ones((8, D), F32)
     for s in range(S):
         k = [keep[s * BLK + 8 * j : s * BLK + 8 * j + 8] for j in range(STEPS)]
@@ -112,20 +133,14 @@
             A = A * An
         carry = jnp.where(i == 0, 0.0, r.scarry[s])
         ends = Q + A * carry
-        start = jnp.where(sub == 0, carry, pltpu.roll(ends, 1, 0))
         r.scarry[s] = jnp.broadcast_to(ends[7:8], (8, D))
-        r.start[i, s] = start
-        Q = start
+        Q = jnp.where(sub == 0, carry, pltpu.roll(ends, 1, 0))
         for j in range(STEPS):
+            at = s * BLK + 8 * j
+            place = pl.ds(pl.multiple_of(i * (S * BLK) + at, 8), 8)
+            r.to_rate[place, :] = bend[at : at + 8] * (gap[at : at + 8] - Q)
             Q = k[j] * Q + d[j]
-            r.state[pl.ds(i * (S * BLK) + s * BLK + 8 * j, 8), :] = Q
-
-
-def live(i, r, dims):
-    S, L, D = dims
-    row = lax.broadcasted_iota(jnp.int32, (BLK, D), 0)
-    time = (row & 7) * STEPS + (row >> 3) + i * BLK
-    return jnp.concatenate([time < r.lengths[s] for s in range(S)], axis=0)
+            r.state[place, :] = Q
 
 
 def normalise(values, D):
@@ -136,50 +151,66 @@
     return c * rs, rs
 
 
-def norm_back(dy, gain, xhat, rs, D):
-    dx = dy * gain
-    m1 = jnp.sum(dx, axis=1, keepdims=True) * (1.0 / D)
-    m2 = jnp.sum(dx * xhat, axis=1, keepdims=True) * (1.0 / D)
-    return rs * (dx - m1 - xhat * m2)
-
-
-def feed_forward(i, r, dims):
+def norms(i, r, dims):
+    S, L, D = dims
+    rows = block_rows(i, dims)
+    xhat1, rs1 = normalise(r.state[rows, :], D)
+    branch = jnp.where(live(i, r, dims), xhat1 * r.g1[...] + r.b1[...], 0.0)
+    mid = r.joined[rows, pl.ds(0, D)].astype(F32) + branch
+    xhat2, rs2 = normalise(mid, D)
+    normed = (xhat2 * r.g2[...] + r.b2[...]).astype(BF16)
+    r.xhat1[rows, :] = xhat1
+    r.xhat2[rows, :] = xhat2
+    r.rs1[rows, :] = rs1
+    r.rs2[rows, :] = rs2
+    r.mid[rows, :] = mid
+    r.normed[rows, :] = normed
+    r.normed_t[pl.ds(0, D), rows] = normed.T
+
+
+def feed_up(i, r, dims):
     S, L, D = dims
     FF = r.wu.shape[1]
     rows = block_rows(i, dims)
-    valid = live(i, r, dims)
-    g1, b1, g2, b2 = r.g1[...], r.b1[...], r.g2[...], r.b2[...]
-    xhat1, rs1 = normalise(r.state[rows, :], D)
-    mid = r.joined[rows, pl.ds(0, D)].astype(F32) + jnp.where(valid, xhat1 * g1 + b1, 0.0)
-    xhat2, rs2 = normalise(mid, D)
-    normed = (xhat2 * g2 + b2).astype(BF16)
-    r.normed[rows, :] = normed
-    r.mid[rows, :] = mid
-    gout = r.gout[rows, :]
-    W = FF_STEP
-    gn = None
-    for n in range(FF // W):
-        cols = slice(n * W, (n + 1) * W)
-        down = r.wd_rows(n, W)
+    normed, half_t = r.normed[rows, :], r.half_t[:, rows]
+    for n in range(FF // FF_STEP):
+        cols = slice(n * FF_STEP, (n + 1) * FF_STEP)
         pu = mm(normed, r.wu[:, cols]) + r.bu[:, cols]
         v2 = pu * pu
-        h = 0.5 * jnp.tanh(pu * (v2 * (GC * GA) + GC)) + 0.5
-        hid = pu * h
-        r.hidden[rows, cols] = hid.astype(BF16)
-        slope = h + hid * (1.0 - h) * (v2 * (6.0 * GA * GC) + 2.0 * GC)
-        gpu = (mm_nt(gout, down) * slope).astype(BF16)
-        r.gpu[rows, cols] = gpu
-        r.gbu[:, cols] += fold(gpu.astype(F32))
-        gnn = mm_nt(gpu, r.wu[:, cols])
-        gn = gnn if gn is None else gn + gnn
-    r.gg2[...] += fold(gn * xhat2)
-    r.gb2[...] += fold(gn)
-    gmid = r.mixed_cot[rows, :].astype(F32) + norm_back(gn, g2, xhat2, rs2, D)
+        s = 1.0 + jnp.tanh(pu * (v2 * (GC * GA) + GC))
+        hid = pu * s
+        hid16 = hid.astype(BF16)
+        r.hidden[rows, cols] = hid16
+        r.slope[rows, cols] = s + hid * (2.0 - s) * (v2 * (3.0 * GA * GC) + GC)
+        r.dwd_t[:, cols] += mm(half_t, hid16)
+
+
+def norm_back(dx, xhat, rs, total, by_gain, D):
+    ex = dx * xhat
+    total[...] += fold(dx)
+    by_gain[...] += fold(ex)
+    m1 = jnp.sum(dx, axis=1, keepdims=True) * (1.0 / D)
+    m2 = jnp.sum(ex, axis=1, keepdims=True) * (1.0 / D)
+    return rs * (dx - m1 - xhat * m2)
+
+
+def feed_down(i, r, dims):
+    S, L, D = dims
+    FF = r.wu.shape[1]
+    rows = block_rows(i, dims)
+    half, normed_t = r.half[rows, :], r.normed_t[:, rows]
+    for n in range(FF // FF_STEP):
+        cols = slice(n * FF_STEP, (n + 1) * FF_STEP)
+        gpu = (mm_nt(half, r.wd_rows(n, FF_STEP)) * r.slope[rows, cols]).astype(BF16)
+        r.gpu[:, cols] = gpu
+        part = mm(normed_t, gpu)
+        add_to(r.dwu, cols, part[:D])
+        r.gbu[:, cols] += part[D : D + 8]
+    gn = mm_nt(r.gpu[...], r.wu[...])
+    gmid = r.mixed_cot[rows, :].astype(F32) + norm_back(gn * r.g2[...], r.xhat2[rows, :], r.rs2[rows, :], r.gb2, r.gg2, D)
     r.gmid[rows, :] = gmid
-    dy1 = jnp.where(valid, gmid, 0.0)
-    r.gg1[...] += fold(dy1 * xhat1)
-    r.gb1[...] += fold(dy1)
-    r.gnorm[rows, :] = norm_back(dy1, g1, xhat1, rs1, D)
+    dx = jnp.where(live(i, r, dims), gmid * r.g1[...], 0.0)
+    r.gnorm[rows, :] = norm_back(dx, r.xhat1[rows, :], r.rs1[rows, :], r.gb1, r.gg1, D)
 
 
 def gates_back(i, r, dims):
@@ -187,11 +218,9 @@
     nb = L // BLK
     rows = block_rows(i, dims)
     sub = sublane((8, D))
-    o = r.o[rows, :]
-    keep = 1.0 - o
+    keep = r.keep[rows, :]
     gnorm = r.gnorm[rows, :]
-    state = r.state[rows, :]
-    gss, sps = [], []
+    gs = []
     one = jnp.ones((8, D), F32)
     for s in range(S):
         k = [keep[s * BLK + 8 * j : s * BLK + 8 * j + 8] for j in range(STEPS)]
@@ -212,33 +241,26 @@
         H = jnp.where(sub == 7, carry, pltpu.roll(ends, 7, 0))
         out = [None] * STEPS
         for j in range(STEPS - 1, -1, -1):
-            G = g[j] + H
-            H = k[j] * G
-            out[j] = G
-        gss += out
-        sps += [r.start[i, s], state[s * BLK : (s + 1) * BLK - 8]]
-    gs = jnp.concatenate(gss, axis=0)
-    sp = jnp.concatenate(sps, axis=0)
-    v = r.v[rows, :]
-    f = r.f[rows, :]
-    go = gs * o
-    grate = go * keep * (v - f - sp)
-    gv = go * (1.0 - v * v)
-    gf = (gs - go) * (1.0 - f * f)
-    gph = jnp.concatenate([grate, gv, gf], axis=1).astype(BF16)
-    r.gph[rows, :] = gph
-    r.gbh[...] += fold(gph.astype(F32))
-    inner = r.inner[rows, :]
-    gpb = (mm_nt(gph, r.wh[...]) * ((1.7159 * 0.666) * (1.0 - inner * inner))).astype(BF16)
+            out[j] = g[j] + H
+            H = k[j] * out[j]
+        gs += out
+    gs = jnp.concatenate(gs, axis=0)
+    gph = jnp.concatenate([gs * r.to_rate[rows, :], gs * r.to_value[rows, :], gs * r.to_fallback[rows, :]], axis=1).astype(BF16)
+    gpb = (mm_nt(gph, r.wh[...]) * r.bend[rows, :]).astype(BF16)
     r.gpb[rows, :] = gpb
-    r.gbb[...] += fold(gpb.astype(F32))
+    part = mm(r.feat_t[:, rows], gph)
+    add_to(r.dwh, slice(0, 3 * D), part[:D])
+    r.gbh[...] += part[D : D + 8]
+    part = mm(r.joined_t[:, rows], gpb)
+    add_to(r.dwb, slice(0, D), part[: 2 * D])
+    r.gbb[...] += part[2 * D : 2 * D + 8]
 
 
 def emit(i, r, dims):
     S, L, D = dims
     rows = block_rows(i, dims)
     back = shuffle(True)
-    branch = mm(r.hidden[rows, :], flat(r.wd)) + r.bd[...]
+    branch = 0.5 * mm(r.hidden[rows, :], flat(r.wd)) + r.bd[...]
     out = (r.mid[rows, :] + jnp.where(live(i, r, dims), branch, 0.0)).astype(BF16)
     for s in range(S):
         r.out[pl.ds(s * L + i * BLK, BLK), :] = mm(back, out[s * BLK : (s + 1) * BLK]).astype(BF16)
@@ -266,10 +288,24 @@
 SUMS = ("gbb", "gbh", "gg1", "gb1", "gg2", "gb2", "gbu", "gbd")
 
 
-def zero_sums(r):
-    for name in SUMS:
+def set_up(r):
+    for name in SUMS + ("dwu", "dwd_t", "dwh", "dwb"):
         ref = getattr(r, name)
         ref[...] = jnp.zeros_like(ref)
+    for ref in (r.joined_t, r.feat_t, r.normed_t):
+        ref[pl.ds(ref.shape[0] - 16, 16), :] = jnp.ones((16, ref.shape[1]), BF16)
+
+
+def column_sums(r):
+    parts = []
+    for name in SUMS:
+        if name in ("gbb", "gbh", "gbu"):
+            parts.append(getattr(r, name)[0:1, :])
+        else:
+            part = jnp.sum(getattr(r, name)[...], axis=0, keepdims=True)
+            gain = {"gg1": r.g1, "gb1": r.g1, "gg2": r.g2, "gb2": r.g2}.get(name)
+            parts.append(part if gain is None else part / gain[...])
+    return jnp.concatenate(parts, axis=1)
 
 
 def sum_widths(D, FF):
@@ -280,11 +316,14 @@
     T = S * L
     v = pltpu.VMEM
     space = dict(
-        joined=v((T, 2 * D), BF16), inner=v((T, D), F32), feat=v((T, D), BF16),
-        o=v((T, D), F32), v=v((T, D), F32), f=v((T, D), F32), state=v((T, D), F32),
-        start=v((L // BLK, S, 8, D), F32), xcarry=v((S, 8, D), F32), scarry=v((S, 8, D), F32),
-        normed=v((T, D), BF16), gout=v((T, D), BF16), hidden=v((T, FF), BF16), gpu=v((T, FF), BF16),
-        mixed_cot=v((T, D), BF16), mid=v((T, D), F32), gmid=v((T, D), F32), gnorm=v((T, D), F32), gph=v((T, 3 * D), BF16), gpb=v((T, D), BF16),
+        joined=v((T, 2 * D), BF16), joined_t=v((2 * D + 16, T), BF16), mixed_cot=v((T, D), BF16),
+        half=v((T, D), BF16), half_t=v((D, T), BF16), bend=v((T, D), F32),
+        feat=v((T, D), BF16), feat_t=v((D + 16, T), BF16), keep=v((T, D), F32),
+        to_rate=v((T, D), F32), to_value=v((T, D), F32), to_fallback=v((T, D), F32), state=v((T, D), F32),
+        xcarry=v((S, 8, D), F32), scarry=v((S, 8, D), F32), xhat1=v((T, D), F32), xhat2=v((T, D), F32),
+        rs1=v((T, 1), F32), rs2=v((T, 1), F32), mid=v((T, D), F32), normed=v((T, D), BF16),
+        normed_t=v((D + 16, T), BF16), hidden=v((T, FF), BF16), slope=v((T, FF), F32),
+        gpu=v((S * BLK, FF), BF16), dwd_t=v((D, FF), F32),
     )
     for name, width in zip(SUMS, sum_widths(D, FF)):
         space[name] = v((8, width), F32)
@@ -304,6 +343,7 @@
     r = Refs()
     for name, ref in zip(names, refs):
         setattr(r, name, ref)
+    r.gnorm, r.gmid, r.gpb = r.state, r.xhat2, r.feat
     return r
 
 
@@ -371,11 +411,26 @@
 
 
 class Share:
-    def __init__(self, r, name, cutter, copies, place):
+    def __init__(self, r, name, cutter, copies, place, plane_first):
         self.r, self.name, self.cut, self.copies, self.p = r, name, cutter, copies, place
+        self.plane_first = plane_first
 
     def ref(self, kind):
         return getattr(self.r, kind + self.name)
+
+    def mine(self, ref):
+        return ref[self.p.z] if self.plane_first else ref[:, self.p.q]
+
+    def send(self, ref, target, along_planes):
+        p, sent = self.p, []
+        for k in range(1, p.planes if along_planes else QUAD):
+            if along_planes:
+                part, device = p.plane(k), p.device(p.plane(k), p.q)
+            else:
+                part, device = p.corner(k), p.device(p.z, p.corner(k))
+            source = ref.at[:, part] if len(ref.shape) == 4 and not along_planes else ref.at[part]
+            sent.append(self.copies.start(source, target.at[k - 1], device))
+        return sent
 
     def pair(self):
         p = self.p
@@ -383,48 +438,43 @@
         self.sent = [self.copies.start(self.ref("cs"), self.ref("cr"), p.partner)]
 
     def spread(self):
-        p = self.p
         arrived(self.sent)
-        total = self.cut(self.ref("dw")[:, :, p.c]) + self.ref("cr")[...].astype(F32)
+        total = self.cut(self.ref("dw")[:, :, self.p.c]) + self.ref("cr")[...].astype(F32)
         self.ref("xs")[...] = total.astype(BF16)
-        self.sent = []
-        for b in range(1, QUAD):
-            q = p.corner(b)
-            self.sent.append(self.copies.start(self.ref("xs").at[:, q], self.ref("xr").at[b - 1], p.device(p.z, q)))
+        self.sent = self.send(self.ref("xs"), self.ref("xr"), self.plane_first)
 
     def climb(self):
         p = self.p
         arrived(self.sent)
-        total = self.cut(self.ref("dw")[:, p.q, p.c]) + self.ref("cr")[:, p.q].astype(F32)
-        for b in range(QUAD - 1):
-            total = total + self.ref("xr")[b].astype(F32)
+        own = self.ref("dw")[p.z, :, p.c] if self.plane_first else self.ref("dw")[:, p.q, p.c]
+        total = self.cut(own) + self.mine(self.ref("cr")).astype(F32)
+        for k in range(len(self.sent)):
+            total = total + self.ref("xr")[k].astype(F32)
         self.ref("ac")[...] = total
         self.ref("zs")[...] = total.astype(BF16)
-        self.sent = []
-        for a in range(1, p.planes):
-            z = p.plane(a)
-            self.sent.append(self.copies.start(self.ref("zs").at[z], self.ref("zr").at[a - 1], p.device(z, p.q)))
+        self.sent = self.send(self.ref("zs"), self.ref("zr"), not self.plane_first)
 
     def land(self):
         arrived(self.sent)
-        total = self.ref("ac")[self.p.z]
-        for k in range(self.p.planes - 1):
+        total = self.ref("ac")[self.p.q if self.plane_first else self.p.z]
+        for k in range(len(self.sent)):
             total = total + self.ref("zr")[k].astype(F32)
         return total
 
 
-def share_space(name, n, rows, columns, cutting):
+def share_space(name, n, rows, columns, cutting, plane_first):
     Z, v = n // (2 * QUAD), pltpu.VMEM
     R, C = (2 * rows, columns // 2) if cutting else (rows, columns)
+    first, second = (Z, QUAD) if plane_first else (QUAD, Z)
     return {
         "dw" + name: v((Z, QUAD, 2, rows, columns), F32),
         "cs" + name: v((Z, QUAD, R, C), BF16),
         "cr" + name: v((Z, QUAD, R, C), BF16),
         "xs" + name: v((Z, QUAD, R, C), BF16),
-        "xr" + name: v((QUAD - 1, Z, R, C), BF16),
-        "ac" + name: v((Z, R, C), F32),
-        "zs" + name: v((Z, R, C), BF16),
-        "zr" + name: v((Z - 1, R, C), BF16),
+        "xr" + name: v((first - 1, second, R, C), BF16),
+        "ac" + name: v((second, R, C), F32),
+        "zs" + name: v((second, R, C), BF16),
+        "zr" + name: v((second - 1, R, C), BF16),
     }
 
 
@@ -456,12 +506,14 @@
 
 
 ROWS = ("gback", "gheads", "gup", "gdown", "gvec")
-INPUTS = ("lengths", "x_hbm", "cot_hbm", "wb_own", "wh_own", "wu_own", "wd_own", "vec_own")
-OUTPUTS = ("out_hbm", "ig_hbm") + ROWS
+OWN = tuple("own_" + name for name in ("bb", "bh", "g1", "b1", "g2", "b2", "bu", "bd"))
+INPUTS = ("lengths", "x_hbm", "cot_hbm", "wb_own", "wh_own", "wu_own", "wd_own") + OWN
+OUTPUTS = ("out", "ig") + ROWS
 
 
 def mega(names, dims, n, FF, *refs):
     r = refs_of(names, refs)
+    r.x, r.cot = r.out, r.ig
     S, L, D = dims
     nb = L // BLK
     p = Place(n)
@@ -471,7 +523,7 @@
         def step(i, c):
             f(nb - 1 - i if down else i, r, dims)
             return c
-        lax.fori_loop(first, last, step, 0)
+        lax.fori_loop(first, last, step, 0, unroll=True)
 
     barrier = pltpu.get_barrier_semaphore()
     for peer in p.peers():
@@ -480,15 +532,22 @@
     loads = [
         pltpu.make_async_copy(src, dst, r.local.at[k])
         for k, (src, dst) in enumerate((
-            (r.wb_own, r.wb.at[p.z, p.q, p.c]), (r.vec_own, r.vec.at[p.c, p.q, pl.ds(p.z, 1)]),
+            (r.wb_own, r.wb.at[p.z, p.q, p.c]),
             (r.wh_own, r.wh_mine), (r.wu_own, r.wu_mine), (r.wd_own, r.wd.at[p.z, p.q, p.c]),
+            *((getattr(r, name), getattr(r, "my_" + name)) for name in OWN),
             (r.x_hbm, r.x), (r.cot_hbm, r.cot),
         ))
     ]
     for load in loads:
         load.start()
-    for load in loads[:5]:
+    r.vec_rows[...] = jnp.zeros_like(r.vec_rows)
+    for load in loads[:-2]:
         load.wait()
+    own_row = jnp.zeros((1, 128), F32)
+    for k, (name, lane, width, own, offset) in enumerate(segments(n, D, FF)):
+        r.vec_rows[pl.ds(k, 1), pl.ds(0, own)] = getattr(r, "my_" + OWN[k])[...].astype(F32)
+        own_row = own_row + pltpu.roll(r.vec_rows[pl.ds(k, 1), :], offset, 1)
+    r.vec[p.c, p.q, pl.ds(p.z, 1)] = own_row
     r.wh_cut[p.z, p.q, p.c] = cut(r.wh_mine[...].astype(F32)).astype(BF16)
     r.wu_cut[p.z, p.q, p.c] = cut(r.wu_mine[...].astype(F32)).astype(BF16)
     pl.semaphore_wait(barrier, len(p.peers()))
@@ -507,15 +566,15 @@
     vec_in = to_planes(r.vec.at[p.c, p.q, pl.ds(p.z, 1)])
     wh_in, up_in, down_in = (to_planes(ref.at[p.z, p.q, p.c]) for ref in weights[1:])
 
-    zero_sums(r)
+    set_up(r)
     arrived(wb_in)
     wb_in = to_corners(r.wb.at[:, p.q, p.c])
     arrived(vec_in)
     vec_in = to_corners(r.vec.at[p.c, p.q])
     arrived(wh_in)
     wh_in = to_corners(r.wh_cut.at[:, p.q, p.c])
-    loads[5].wait()
-    loads[6].wait()
+    for load in loads[-2:]:
+        load.wait()
     run(enter, 0, nb)
     fill_pick(r, n, D, FF)
     arrived(wb_in)
@@ -541,32 +600,32 @@
     run(gates, 0, nb)
     arrived(up_in)
     up_in = to_partner(r.wu_cut.at[:, :, p.c])
+    run(norms, 0, nb)
+    arrived(up_in)
+    r.wu[...] = uncut(r.wu_cut[...].astype(F32)).reshape(D, FF).astype(BF16)
+    run(feed_up, 0, 1)
     arrived(down_in)
     down_in = to_partner(r.wd.at[:, :, p.c])
-    arrived(up_in)
-    r.wu[...] = uncut(r.wu_cut[...].astype(F32)).reshape(D, FF).astype(BF16)
+    run(feed_up, 1, nb)
     arrived(down_in)
-    run(feed_forward, 0, nb)
-
-    up = Share(r, "u", cut, copies, p)
-    down = Share(r, "d", same, copies, p)
-    heads = Share(r, "h", cut, copies, p)
-    back = Share(r, "b", same, copies, p)
-    r.dwu[...] = mm_tn(r.normed[...], r.gpu[...]).reshape(r.dwu.shape)
+
+    up = Share(r, "u", cut, copies, p, UP_PLANE)
+    down = Share(r, "d", same, copies, p, DOWN_PLANE)
+    heads = Share(r, "h", cut, copies, p, HEADS_PLANE)
+    back = Share(r, "b", same, copies, p, BACK_PLANE)
+    r.dwd[...] = r.dwd_t[...].T.reshape(r.dwd.shape)
+    down.pair()
+    run(feed_down, 0, 2)
+    down.spread()
+    run(feed_down, 2, nb)
     up.pair()
-    r.dwd[...] = mm_tn(r.gout[...], r.hidden[...]).T.reshape(r.dwd.shape)
-    down.pair()
-    run(gates_back, 0, 1, True)
+    run(gates_back, 0, 2, True)
     up.spread()
-    down.spread()
-    run(gates_back, 1, nb, True)
-    r.dwh[...] = mm_tn(r.feat[...], r.gph[...]).reshape(r.dwh.shape)
+    run(gates_back, 2, nb, True)
     heads.pair()
-    r.dwb[...] = mm_tn(r.gpb[...], r.joined[...]).T.reshape(r.dwb.shape)
     back.pair()
 
-    sums = jnp.concatenate([jnp.sum(getattr(r, name)[...], axis=0, keepdims=True) for name in SUMS], axis=1)
-    rest, rows = jnp.where(owners(n, D, FF), sums, 0.0), None
+    rest, rows = jnp.where(owners(n, D, FF), column_sums(r), 0.0), None
     for _ in range(3):
         part = rest.astype(BF16)
         rest = rest - part.astype(F32)
@@ -582,11 +641,9 @@
     for b in range(1, QUAD):
         q = p.corner(b)
         vec_out.append(copies.start(r.va.at[q], r.vx.at[b - 1], p.device(p.z, q)))
+    down.climb()
     up.climb()
-    down.climb()
     run(leave, 0, nb, True)
-    outs = [pltpu.make_async_copy(r.ig, r.ig_hbm, r.local.at[7])]
-    outs[0].start()
     heads.climb()
     back.climb()
     arrived(vec_out)
@@ -599,8 +656,6 @@
         z = p.plane(a)
         vec_out.append(copies.start(r.vz.at[pl.ds(z, 1)], r.vt.at[pl.ds(a - 1, 1)], p.device(z, p.q)))
     run(emit, 0, nb)
-    outs.append(pltpu.make_async_copy(r.out, r.out_hbm, r.local.at[8]))
-    outs[1].start()
     r.gup[...] = uncut(up.land())
     r.gdown[...] = down.land()
     r.gheads[...] = uncut(heads.land())
@@ -608,11 +663,10 @@
     arrived(vec_out)
     r.gvec[...] = r.vz[pl.ds(p.z, 1), :] + jnp.sum(r.vt[...], axis=0, keepdims=True)
     copies.finish()
-    for out in outs:
-        out.wait()
 
 
 def quick(lengths, x, cot, wb, wh, wu, wd, vectors, n):
+    vectors = [v.reshape(1, -1) for v in vectors]
     S = lengths.shape[0]
     T, D = x.shape
     L, FF = T // S, wu.shape[1]
@@ -620,83 +674,64 @@
     space = work_space(S, L, D, FF)
     rb, rh, ru, rd = wb.shape[0], wh.shape[0], wu.shape[0], wd.shape[0]
     space.update(
-        x=v((T, D), BF16), cot=v((T, D), BF16), out=v((T, D), BF16), ig=v((T, D), BF16),
         wb=v((Z, QUAD, 2, rb, D), BF16), wd=v((Z, QUAD, 2, rd, D), BF16),
         wh_cut=v((Z, QUAD, 2, 2 * rh, 3 * D // 2), BF16), wu_cut=v((Z, QUAD, 2, 2 * ru, FF // 2), BF16),
         wh=v((D, 3 * D), BF16), wu=v((D, FF), BF16), wh_mine=v((rh, 3 * D), BF16), wu_mine=v((ru, FF), BF16),
         vec=v((2, QUAD, Z, 128), F32), pick=v((sum(sum_widths(D, FF)), 128), BF16),
         vs=v((2, QUAD, Z, 128), F32), vr=v((QUAD, Z, 128), F32), va=v((QUAD, Z, 128), F32),
         vx=v((QUAD - 1, Z, 128), F32), vz=v((Z, 128), F32), vt=v((Z - 1, 128), F32),
-        local=pltpu.SemaphoreType.DMA((9,)), send=pltpu.SemaphoreType.DMA((72,)), recv=pltpu.SemaphoreType.DMA((72,)),
+        local=pltpu.SemaphoreType.DMA((14,)), send=pltpu.SemaphoreType.DMA((72,)), recv=pltpu.SemaphoreType.DMA((72,)),
     )
     for name, lane, width, own, offset in segments(n, D, FF):
         space[name] = v((1, width), F32)
-    space.update(share_space("u", n, ru, FF, True))
-    space.update(share_space("d", n, rd, D, False))
-    space.update(share_space("h", n, rh, 3 * D, True))
-    space.update(share_space("b", n, rb, D, False))
-    row = lambda a, b: jax.ShapeDtypeStruct((a, b), F32)
+        space["my_own_" + name] = v((1, own), BF16)
+    space["vec_rows"] = v((8, 128), F32)
+    space.update(share_space("u", n, ru, FF, True, UP_PLANE))
+    space.update(share_space("d", n, rd, D, False, DOWN_PLANE))
+    space.update(share_space("h", n, rh, 3 * D, True, HEADS_PLANE))
+    space.update(share_space("b", n, rb, D, False, BACK_PLANE))
     shapes = (
-        jax.ShapeDtypeStruct((T, D), BF16), jax.ShapeDtypeStruct((T, D), BF16),
-        row(rb, D), row(rh, 3 * D), row(ru, FF), row(rd, D), row(1, 128),
+        v((T, D), BF16), v((T, D), BF16),
+        v((rb, D), F32), v((rh, 3 * D), F32), v((ru, FF), F32), v((rd, D), F32), v((1, 128), F32),
     )
     hbm, vmem = pl.BlockSpec(memory_space=pl.ANY), pl.BlockSpec(memory_space=pltpu.VMEM)
     results = pl.pallas_call(
         functools.partial(mega, INPUTS + OUTPUTS + tuple(space), (S, L, D), n, FF),
         out_shape=shapes,
-        in_specs=[pl.BlockSpec(memory_space=pltpu.SMEM)] + [hbm] * 7,
-        out_specs=[hbm] * 2 + [vmem] * 5,
+        in_specs=[pl.BlockSpec(memory_space=pltpu.SMEM)] + [hbm] * 14,
+        out_specs=[vmem] * 7,
         scratch_shapes=list(space.values()),
-        compiler_params=pltpu.CompilerParams(collective_id=0, has_side_effects=True, vmem_limit_bytes=62 << 20),
-    )(lengths, x, cot, wb, wh, wu, wd, vectors)
+        compiler_params=pltpu.CompilerParams(collective_id=0, has_side_effects=True, vmem_limit_bytes=60 << 20),
+    )(lengths, x, cot, wb, wh, wu, wd, *vectors)
     return hand_over(results, [own for name, lane, width, own, offset in segments(n, D, FF)])
 
 
-def hand_over_kernel(widths, parts, *refs):
-    count = len(parts)
-    sources, targets = refs[: count + 1], refs[count + 1 : 2 * count + 1]
-    smalls = refs[2 * count + 1 : 2 * count + 1 + len(widths)]
-    stages, sem_in, sem_out = refs[-count - 3 : -2], refs[-2], refs[-1]
-    moves, k = [], 0
-    for source, stage, cuts in zip(sources, stages, (1,) + parts):
-        rows = source.shape[0] // cuts
-        for j in range(cuts):
-            piece = pl.ds(j * rows, rows)
-            move = pltpu.make_async_copy(source.at[piece], stage.at[piece], sem_in.at[k])
-            move.start()
-            moves.append((move, stage.at[piece], piece))
-            k += 1
-    moves[0][0].wait()
+def hand_over_kernel(widths, *refs):
+    count = 6
+    sources, vec, targets = refs[:count], refs[count], refs[count + 1 : 2 * count + 1]
+    smalls, sem = refs[2 * count + 1 : -1], refs[-1]
+    moves = [pltpu.make_async_copy(s, t, sem.at[k]) for k, (s, t) in enumerate(zip(sources, targets))]
+    for move in moves:
+        move.start()
     at = 0
     for small, width in zip(smalls, widths):
-        small[...] = pltpu.roll(stages[0][...], (128 - at) % 128, 1)[:, :width]
+        small[...] = pltpu.roll(vec[...], (128 - at) % 128, 1)[:, :width]
         at += width
-    k, out = 1, []
-    for target, cuts in zip(targets, parts):
-        for j in range(cuts):
-            move, stage, piece = moves[k]
-            move.wait()
-            out.append(pltpu.make_async_copy(stage, target.at[piece], sem_out.at[k - 1]))
-            out[-1].start()
-            k += 1
-    for move in out:
+    for move in moves:
         move.wait()
 
 
 def hand_over(results, widths):
     hbm, vmem = pl.BlockSpec(memory_space=pl.ANY), pl.BlockSpec(memory_space=pltpu.VMEM)
-    results = results[6:] + results[:6]
-    parts = (4, 4, 1, 1, 1, 1)
-    shapes = [jax.ShapeDtypeStruct(a.shape, a.dtype) for a in results[1:]]
+    shapes = [jax.ShapeDtypeStruct(a.shape, a.dtype) for a in results[:6]]
     shapes += [jax.ShapeDtypeStruct((1, w), F32) for w in widths]
     return pl.pallas_call(
-        functools.partial(hand_over_kernel, widths, parts),
+        functools.partial(hand_over_kernel, widths),
         out_shape=shapes,
-        in_specs=[hbm] * len(results),
-        out_specs=[hbm] * len(parts) + [vmem] * len(widths),
-        scratch_shapes=[pltpu.VMEM(a.shape, a.dtype) for a in results]
-        + [pltpu.SemaphoreType.DMA((sum(parts) + 1,)), pltpu.SemaphoreType.DMA((sum(parts),))],
-        compiler_params=pltpu.CompilerParams(vmem_limit_bytes=62 << 20),
+        in_specs=[vmem] * 7,
+        out_specs=[hbm] * 6 + [vmem] * len(widths),
+        scratch_shapes=[pltpu.SemaphoreType.DMA((6,))],
+        compiler_params=pltpu.CompilerParams(vmem_limit_bytes=16 << 20),
     )(*results)
 
 
@@ -711,18 +746,17 @@
             return c
         lax.fori_loop(0, nb, step, 0)
 
-    zero_sums(r)
-    for f in (enter, backbone, gates, feed_forward):
+    set_up(r)
+    for f in (enter, backbone, gates, norms, feed_up, feed_down, emit):
         run(f)
-    r.gup[...] = mm_tn(r.normed[...], r.gpu[...])
-    r.gdown[...] = mm_tn(r.gout[...], r.hidden[...]).T
-    run(emit)
     run(gates_back, True)
-    r.gheads[...] = mm_tn(r.feat[...], r.gph[...])
-    r.gback[...] = mm_tn(r.gpb[...], r.joined[...]).T
     run(leave, True)
+    r.gdown[...] = r.dwd_t[...].T
+    sums, at = column_sums(r), 0
     for name in SUMS:
-        getattr(r, "all" + name)[...] = jnp.sum(getattr(r, name)[...], axis=0, keepdims=True)
+        ref = getattr(r, "all" + name)
+        ref[...] = sums[:, at : at + ref.shape[1]]
+        at += ref.shape[1]
 
 
 def whole(lengths, x, cot, matrices, vectors):
@@ -731,7 +765,7 @@
     L, FF = T // S, matrices[2].shape[1]
     space = work_space(S, L, D, FF)
     names = ("lengths", "x", "cot", "wb", "wh", "wu", "wd", "bb", "bh", "g1", "b1", "g2", "b2", "bu", "bd")
-    names += ("out", "ig") + ROWS[:4] + tuple("all" + name for name in SUMS) + tuple(space)
+    names += ("out", "ig", "dwb", "dwh", "dwu", "gdown") + tuple("all" + name for name in SUMS) + tuple(space)
     row = lambda a, b: jax.ShapeDtypeStruct((a, b), F32)
     shapes = (jax.ShapeDtypeStruct((T, D), BF16),) * 2
     shapes += tuple(row(*m.shape) for m in matrices) + tuple(row(1, width) for width in sum_widths(D, FF))
@@ -754,9 +788,7 @@
 
 
 def by_kernel(lengths, x, cot, matrices, vectors, n):
-    used = sum(v.shape[0] for v in vectors)
-    row = jnp.concatenate(vectors + (jnp.zeros((128 - used,), BF16),)).astype(F32).reshape(1, 128)
-    results = quick(lengths, x, cot, *matrices, row, n)
+    results = quick(lengths, x, cot, *matrices, vectors, n)
     return results[:2], results[2:6], [row[0] for row in results[6:]]
 
 

time: 58.2 us -> 51.4 us (0.88)
  Pallas kernels: 55.9 us -> 50.4 us
  local copies, waits for them, and re-layouts: 0.79 us -> 0 us
    pallas_call x1, Pallas kernels: 52.9 us -> 48.4 us  [quick(): pl.pallas_call(functools.partial(mega, INPUTS + OUTPUTS + tuple(space), (...]
    pallas_call x1, Pallas kernels: 3.05 us -> 1.93 us  [hand_over(): pl.pallas_call(functools.partial(hand_over_kernel, widths), out_shape=sha...]
    unnamed x16 -> x0, local copies, waits for them, and re-layouts: 0.69 us -> none
where the time goes in v3:
time: 51.4 us; the launch traced here: 51.2 us
  Pallas kernels  50.4 us (98%)
  between operations  0.82 us (2%)
    pallas_call x1, Pallas kernels, quick(): pl.pallas_call(functools.partial(mega, INPUTS + OUTPUTS + tuple(space), (...  48.4 us
    pallas_call x1, Pallas kernels, hand_over(): pl.pallas_call(functools.partial(hand_over_kernel, widths), out_shape=sha...  1.93 us

profile of v3, /device:TPU:0, one launch (start us, length us, event | category | flops | bytes accessed | tf_op | source)
XLA Modules:
  0.0 51.2 jit_solution(5559850298943823587)
XLA Ops:
  0.7 48.4 %shard_map.254 = (bf16[2048,256]{1,0:T(8,128)(2,1)S(1)}, bf16[2048,256]{1,0:T(8,128)(2,1)S(1)}, f32[16,256]{1,0:T(8,128)S(1)}, f32[8,768]{1,0:T(8,128)S(1)}, f32...) custom-call(s32[2]{0:T(128)} %refs_0_.1, bf16[2048,256]{1,0:T(8,128)(2,1)} %refs_1_.1, ...), custom_call_target="tpu_custom_call" | custom-call | tf_op jit(solution)/shard_map/pallas_call | solution.py:698
  49.1 1.9 %shard_map.255 = (bf16[2048,256]{1,0:T(8,128)(2,1)}, bf16[2048,256]{1,0:T(8,128)(2,1)}, f32[16,256]{1,0:T(8,128)}, f32[8,768]{1,0:T(8,128)}, f32[8,1024]{1,0:T(8...) custom-call(bf16[2048,256]{1,0:T(8,128)(2,1)S(1)} %get-tuple-element, ...), custom_call_target="tpu_custom_call" | custom-call | tf_op jit(solution)/shard_map/pallas_call | solution.py:728

commit v4 on v3

--- a/solution.py
+++ b/solution.py
@@ -168,21 +168,26 @@
     r.normed_t[pl.ds(0, D), rows] = normed.T
 
 
-def feed_up(i, r, dims):
-    S, L, D = dims
-    FF = r.wu.shape[1]
-    rows = block_rows(i, dims)
-    normed, half_t = r.normed[rows, :], r.half_t[:, rows]
-    for n in range(FF // FF_STEP):
-        cols = slice(n * FF_STEP, (n + 1) * FF_STEP)
-        pu = mm(normed, r.wu[:, cols]) + r.bu[:, cols]
-        v2 = pu * pu
-        s = 1.0 + jnp.tanh(pu * (v2 * (GC * GA) + GC))
-        hid = pu * s
-        hid16 = hid.astype(BF16)
-        r.hidden[rows, cols] = hid16
-        r.slope[rows, cols] = s + hid * (2.0 - s) * (v2 * (3.0 * GA * GC) + GC)
-        r.dwd_t[:, cols] += mm(half_t, hid16)
+def feed_up(i, n, r, dims):
+    rows, cols = block_rows(i, dims), slice(n * FF_STEP, (n + 1) * FF_STEP)
+    pu = mm(r.normed[rows, :], r.wu[:, cols]) + r.bu[:, cols]
+    v2 = pu * pu
+    s = 1.0 + jnp.tanh(pu * (v2 * (GC * GA) + GC))
+    hid = pu * s
+    hid16 = hid.astype(BF16)
+    r.hidden[rows, cols] = hid16
+    r.slope[i % 2, :, cols] = s + hid * (2.0 - s) * (v2 * (3.0 * GA * GC) + GC)
+    r.dwd_t[:, cols] += mm(r.half_t[:, rows], hid16)
+
+
+def feed_down(i, n, r, dims):
+    D = dims[2]
+    rows, cols = block_rows(i, dims), slice(n * FF_STEP, (n + 1) * FF_STEP)
+    gpu = (mm_nt(r.half[rows, :], r.wd_rows(n, FF_STEP)) * r.slope[i % 2, :, cols]).astype(BF16)
+    r.gpu[i % 2, :, cols] = gpu
+    part = mm(r.normed_t[:, rows], gpu)
+    add_to(r.dwu, cols, part[:D])
+    r.gbu[:, cols] += part[D : D + 8]
 
 
 def norm_back(dx, xhat, rs, total, by_gain, D):
@@ -194,19 +199,10 @@
     return rs * (dx - m1 - xhat * m2)
 
 
-def feed_down(i, r, dims):
-    S, L, D = dims
-    FF = r.wu.shape[1]
+def norms_back(i, r, dims):
+    S, L, D = dims
     rows = block_rows(i, dims)
-    half, normed_t = r.half[rows, :], r.normed_t[:, rows]
-    for n in range(FF // FF_STEP):
-        cols = slice(n * FF_STEP, (n + 1) * FF_STEP)
-        gpu = (mm_nt(half, r.wd_rows(n, FF_STEP)) * r.slope[rows, cols]).astype(BF16)
-        r.gpu[:, cols] = gpu
-        part = mm(normed_t, gpu)
-        add_to(r.dwu, cols, part[:D])
-        r.gbu[:, cols] += part[D : D + 8]
-    gn = mm_nt(r.gpu[...], r.wu[...])
+    gn = mm_nt(r.gpu[i % 2], r.wu[...])
     gmid = r.mixed_cot[rows, :].astype(F32) + norm_back(gn * r.g2[...], r.xhat2[rows, :], r.rs2[rows, :], r.gb2, r.gg2, D)
     r.gmid[rows, :] = gmid
     dx = jnp.where(live(i, r, dims), gmid * r.g1[...], 0.0)
@@ -256,6 +252,25 @@
     r.gbb[...] += part[2 * D : 2 * D + 8]
 
 
+def middle(r, dims, after):
+    nb = dims[1] // BLK
+    for step in range(nb + 1):
+        for n in range(r.wu.shape[1] // FF_STEP):
+            if step < nb:
+                feed_up(nb - 1 - step, n, r, dims)
+            if 0 <= step - 1 < nb:
+                feed_down(nb - 1 - (step - 1), n, r, dims)
+        if step:
+            norms_back(nb - step, r, dims)
+        for action in after.get(step, ()):
+            action()
+    for i in reversed(range(nb)):
+        gates_back(i, r, dims)
+        if i == nb // 2:
+            for action in after.get(nb + 1, ()):
+                action()
+
+
 def emit(i, r, dims):
     S, L, D = dims
     rows = block_rows(i, dims)
@@ -322,8 +337,8 @@
         to_rate=v((T, D), F32), to_value=v((T, D), F32), to_fallback=v((T, D), F32), state=v((T, D), F32),
         xcarry=v((S, 8, D), F32), scarry=v((S, 8, D), F32), xhat1=v((T, D), F32), xhat2=v((T, D), F32),
         rs1=v((T, 1), F32), rs2=v((T, 1), F32), mid=v((T, D), F32), normed=v((T, D), BF16),
-        normed_t=v((D + 16, T), BF16), hidden=v((T, FF), BF16), slope=v((T, FF), F32),
-        gpu=v((S * BLK, FF), BF16), dwd_t=v((D, FF), F32),
+        normed_t=v((D + 16, T), BF16), hidden=v((T, FF), BF16), slope=v((2, S * BLK, FF), F32),
+        gpu=v((2, S * BLK, FF), BF16), dwd_t=v((D, FF), F32),
     )
     for name, width in zip(SUMS, sum_widths(D, FF)):
         space[name] = v((8, width), F32)
@@ -374,27 +389,90 @@
 
 class Copies:
     def __init__(self, send, recv):
-        self.send, self.recv, self.used, self.open = send, recv, 0, []
-
-    def start(self, src, dst, device):
-        k = self.used
-        self.used += 1
-        copy = pltpu.make_async_remote_copy(
+        self.send, self.recv, self.groups = send, recv, 0
+        self.open = []
+
+    def group(self, whole):
+        k = self.groups
+        self.groups += 1
+        self.open.append((whole, k))
+        return k
+
+    def copy(self, k, src, dst, device):
+        return pltpu.make_async_remote_copy(
             src_ref=src, dst_ref=dst, send_sem=self.send.at[k], recv_sem=self.recv.at[k],
             device_id=(device,), device_id_type=MESH,
         )
-        copy.start()
-        self.open.append(copy)
-        return copy
+
+    def start(self, k, src, dst, device):
+        self.copy(k, src, dst, device).start()
+
+    def arrived(self, k):
+        whole, _ = self.open[k]
+        self.copy(k, whole, whole, lax.axis_index("dp")).wait_recv()
 
     def finish(self):
-        for copy in self.open:
-            copy.wait_send()
-
-
-def arrived(copies):
-    for copy in copies:
-        copy.wait_recv()
+        for whole, k in self.open:
+            self.copy(k, whole, whole, lax.axis_index("dp")).wait_send()
+
+
+class Gather:
+    def __init__(self, ref, copies, place):
+        self.ref, self.copies, self.p = ref, copies, place
+
+    def begin(self, own):
+        ref, p = self.ref, self.p
+        self.first = self.copies.group(ref.at[pl.ds(0, p.planes - 1), p.q, p.c])
+        self.second = self.copies.group(ref.at[:, pl.ds(0, QUAD - 1), p.c])
+        for a in range(1, p.planes):
+            self.copies.start(self.first, own, ref.at[p.z, p.q, p.c], p.device(p.plane(a), p.q))
+        for b in range(1, QUAD):
+            self.copies.start(self.second, own, ref.at[p.z, p.q, p.c], p.device(p.z, p.corner(b)))
+
+    def spread(self):
+        ref, p = self.ref, self.p
+        self.copies.arrived(self.first)
+        for a in range(1, p.planes):
+            part = ref.at[p.plane(a), p.q, p.c]
+            for b in range(1, QUAD):
+                self.copies.start(self.second, part, part, p.device(p.z, p.corner(b)))
+
+    def pair(self):
+        part = self.ref.at[:, :, self.p.c]
+        self.copies.arrived(self.second)
+        self.third = self.copies.group(part)
+        self.copies.start(self.third, part, part, self.p.partner)
+
+    def end(self):
+        self.copies.arrived(self.third)
+
+
+class GatherRows:
+    def __init__(self, ref, copies, place):
+        self.ref, self.copies, self.p = ref, copies, place
+
+    def begin(self):
+        ref, p = self.ref, self.p
+        self.now = self.copies.group(ref.at[p.c, p.q, pl.ds(0, p.planes - 1)])
+        own = ref.at[p.c, p.q, pl.ds(p.z, 1)]
+        for a in range(1, p.planes):
+            self.copies.start(self.now, own, own, p.device(p.plane(a), p.q))
+
+    def spread(self):
+        ref, p = self.ref, self.p
+        self.end()
+        self.now = self.copies.group(ref.at[p.c, pl.ds(0, QUAD - 1)])
+        for b in range(1, QUAD):
+            self.copies.start(self.now, ref.at[p.c, p.q], ref.at[p.c, p.q], p.device(p.z, p.corner(b)))
+
+    def pair(self):
+        part = self.ref.at[self.p.c]
+        self.end()
+        self.now = self.copies.group(part)
+        self.copies.start(self.now, part, part, self.p.partner)
+
+    def end(self):
+        self.copies.arrived(self.now)
 
 
 def cut(values):
@@ -422,42 +500,43 @@
         return ref[self.p.z] if self.plane_first else ref[:, self.p.q]
 
     def send(self, ref, target, along_planes):
-        p, sent = self.p, []
+        p = self.p
+        self.now = self.copies.group(target)
         for k in range(1, p.planes if along_planes else QUAD):
             if along_planes:
                 part, device = p.plane(k), p.device(p.plane(k), p.q)
             else:
                 part, device = p.corner(k), p.device(p.z, p.corner(k))
             source = ref.at[:, part] if len(ref.shape) == 4 and not along_planes else ref.at[part]
-            sent.append(self.copies.start(source, target.at[k - 1], device))
-        return sent
+            self.copies.start(self.now, source, target.at[k - 1], device)
 
     def pair(self):
         p = self.p
         self.ref("cs")[...] = self.cut(self.ref("dw")[:, :, 1 - p.c]).astype(BF16)
-        self.sent = [self.copies.start(self.ref("cs"), self.ref("cr"), p.partner)]
+        self.now = self.copies.group(self.ref("cr"))
+        self.copies.start(self.now, self.ref("cs"), self.ref("cr"), p.partner)
 
     def spread(self):
-        arrived(self.sent)
+        self.copies.arrived(self.now)
         total = self.cut(self.ref("dw")[:, :, self.p.c]) + self.ref("cr")[...].astype(F32)
         self.ref("xs")[...] = total.astype(BF16)
-        self.sent = self.send(self.ref("xs"), self.ref("xr"), self.plane_first)
+        self.send(self.ref("xs"), self.ref("xr"), self.plane_first)
 
     def climb(self):
         p = self.p
-        arrived(self.sent)
+        self.copies.arrived(self.now)
         own = self.ref("dw")[p.z, :, p.c] if self.plane_first else self.ref("dw")[:, p.q, p.c]
         total = self.cut(own) + self.mine(self.ref("cr")).astype(F32)
-        for k in range(len(self.sent)):
+        for k in range(self.ref("xr").shape[0]):
             total = total + self.ref("xr")[k].astype(F32)
         self.ref("ac")[...] = total
         self.ref("zs")[...] = total.astype(BF16)
-        self.sent = self.send(self.ref("zs"), self.ref("zr"), not self.plane_first)
+        self.send(self.ref("zs"), self.ref("zr"), not self.plane_first)
 
     def land(self):
-        arrived(self.sent)
+        self.copies.arrived(self.now)
         total = self.ref("ac")[self.p.q if self.plane_first else self.p.z]
-        for k in range(len(self.sent)):
+        for k in range(self.ref("zr").shape[0]):
             total = total + self.ref("zr")[k].astype(F32)
         return total
 
@@ -532,16 +611,20 @@
     loads = [
         pltpu.make_async_copy(src, dst, r.local.at[k])
         for k, (src, dst) in enumerate((
-            (r.wb_own, r.wb.at[p.z, p.q, p.c]),
-            (r.wh_own, r.wh_mine), (r.wu_own, r.wu_mine), (r.wd_own, r.wd.at[p.z, p.q, p.c]),
+            (r.wh_own, r.wh_mine), (r.wu_own, r.wu_mine),
             *((getattr(r, name), getattr(r, "my_" + name)) for name in OWN),
+            (r.wb_own, r.wb.at[p.z, p.q, p.c]), (r.wd_own, r.wd.at[p.z, p.q, p.c]),
             (r.x_hbm, r.x), (r.cot_hbm, r.cot),
         ))
     ]
     for load in loads:
         load.start()
+    wb, wh, wu, wd = (Gather(ref, copies, p) for ref in (r.wb, r.wh_cut, r.wu_cut, r.wd))
+    vec = GatherRows(r.vec, copies, p)
+    pl.semaphore_wait(barrier, len(p.peers()))
+    wb.begin(r.wb_own)
     r.vec_rows[...] = jnp.zeros_like(r.vec_rows)
-    for load in loads[:-2]:
+    for load in loads[:-4]:
         load.wait()
     own_row = jnp.zeros((1, 128), F32)
     for k, (name, lane, width, own, offset) in enumerate(segments(n, D, FF)):
@@ -550,78 +633,53 @@
     r.vec[p.c, p.q, pl.ds(p.z, 1)] = own_row
     r.wh_cut[p.z, p.q, p.c] = cut(r.wh_mine[...].astype(F32)).astype(BF16)
     r.wu_cut[p.z, p.q, p.c] = cut(r.wu_mine[...].astype(F32)).astype(BF16)
-    pl.semaphore_wait(barrier, len(p.peers()))
-
-    def to_planes(own):
-        return [copies.start(own, own, p.device(p.plane(a), p.q)) for a in range(1, p.planes)]
-
-    def to_corners(own):
-        return [copies.start(own, own, p.device(p.z, p.corner(b))) for b in range(1, QUAD)]
-
-    def to_partner(own):
-        return [copies.start(own, own, p.partner)]
-
-    weights = (r.wb, r.wh_cut, r.wu_cut, r.wd)
-    wb_in = to_planes(r.wb.at[p.z, p.q, p.c])
-    vec_in = to_planes(r.vec.at[p.c, p.q, pl.ds(p.z, 1)])
-    wh_in, up_in, down_in = (to_planes(ref.at[p.z, p.q, p.c]) for ref in weights[1:])
-
+    vec.begin()
+    wh.begin(r.wh_cut.at[p.z, p.q, p.c])
     set_up(r)
-    arrived(wb_in)
-    wb_in = to_corners(r.wb.at[:, p.q, p.c])
-    arrived(vec_in)
-    vec_in = to_corners(r.vec.at[p.c, p.q])
-    arrived(wh_in)
-    wh_in = to_corners(r.wh_cut.at[:, p.q, p.c])
-    for load in loads[-2:]:
+    wb.spread()
+    vec.spread()
+    wh.spread()
+    wu.begin(r.wu_cut.at[p.z, p.q, p.c])
+    wd.begin(r.wd_own)
+    for load in loads[-4:]:
         load.wait()
     run(enter, 0, nb)
     fill_pick(r, n, D, FF)
-    arrived(wb_in)
-    wb_in = to_partner(r.wb.at[:, :, p.c])
-    arrived(vec_in)
-    vec_in = to_partner(r.vec.at[p.c])
-    arrived(up_in)
-    up_in = to_corners(r.wu_cut.at[:, p.q, p.c])
-    arrived(down_in)
-    down_in = to_corners(r.wd.at[:, p.q, p.c])
-    arrived(wb_in)
-    arrived(vec_in)
+    wb.pair()
+    vec.pair()
+    wu.spread()
+    wd.spread()
+    wb.end()
+    vec.end()
     spread = mm_nt(r.vec[...].reshape(n, 128).astype(BF16), r.pick[...])
     vectors = jnp.sum(jnp.where(owners(n, D, FF), spread, 0.0), axis=0, keepdims=True)
     for name, lane, width, own, offset in segments(n, D, FF):
         getattr(r, name)[...] = vectors[:, lane : lane + width]
 
-    arrived(wh_in)
-    wh_in = to_partner(r.wh_cut.at[:, :, p.c])
     run(backbone, 0, nb)
-    arrived(wh_in)
+    wh.pair()
+    wh.end()
     r.wh[...] = uncut(r.wh_cut[...].astype(F32)).reshape(D, 3 * D).astype(BF16)
     run(gates, 0, nb)
-    arrived(up_in)
-    up_in = to_partner(r.wu_cut.at[:, :, p.c])
+    wu.pair()
     run(norms, 0, nb)
-    arrived(up_in)
+    wu.end()
     r.wu[...] = uncut(r.wu_cut[...].astype(F32)).reshape(D, FF).astype(BF16)
-    run(feed_up, 0, 1)
-    arrived(down_in)
-    down_in = to_partner(r.wd.at[:, :, p.c])
-    run(feed_up, 1, nb)
-    arrived(down_in)
-
+    wd.pair()
     up = Share(r, "u", cut, copies, p, UP_PLANE)
     down = Share(r, "d", same, copies, p, DOWN_PLANE)
     heads = Share(r, "h", cut, copies, p, HEADS_PLANE)
     back = Share(r, "b", same, copies, p, BACK_PLANE)
-    r.dwd[...] = r.dwd_t[...].T.reshape(r.dwd.shape)
-    down.pair()
-    run(feed_down, 0, 2)
-    down.spread()
-    run(feed_down, 2, nb)
-    up.pair()
-    run(gates_back, 0, 2, True)
-    up.spread()
-    run(gates_back, 2, nb, True)
+
+    def turn_down():
+        r.dwd[...] = r.dwd_t[...].T.reshape(r.dwd.shape)
+
+    middle(r, dims, {
+        0: (wd.end,),
+        nb - 1: (turn_down, down.pair),
+        nb: (up.pair, down.spread),
+        nb + 1: (up.spread,),
+    })
     heads.pair()
     back.pair()
 
@@ -632,35 +690,36 @@
         row = mm(part, r.pick[...])
         rows = row if rows is None else rows + row
     r.vs[...] = rows.reshape(r.vs.shape)
-    vec_out = [copies.start(r.vs.at[1 - p.c], r.vr, p.partner)]
+    vec_out = copies.group(r.vr)
+    copies.start(vec_out, r.vs.at[1 - p.c], r.vr, p.partner)
     heads.spread()
     back.spread()
-    arrived(vec_out)
+    copies.arrived(vec_out)
     r.va[...] = r.vs[p.c] + r.vr[...]
-    vec_out = []
+    vec_out = copies.group(r.vx)
     for b in range(1, QUAD):
         q = p.corner(b)
-        vec_out.append(copies.start(r.va.at[q], r.vx.at[b - 1], p.device(p.z, q)))
+        copies.start(vec_out, r.va.at[q], r.vx.at[b - 1], p.device(p.z, q))
     down.climb()
     up.climb()
     run(leave, 0, nb, True)
     heads.climb()
     back.climb()
-    arrived(vec_out)
+    copies.arrived(vec_out)
     total = r.va[p.q]
     for b in range(QUAD - 1):
         total = total + r.vx[b]
     r.vz[...] = total
-    vec_out = []
+    vec_out = copies.group(r.vt)
     for a in range(1, p.planes):
         z = p.plane(a)
-        vec_out.append(copies.start(r.vz.at[pl.ds(z, 1)], r.vt.at[pl.ds(a - 1, 1)], p.device(z, p.q)))
+        copies.start(vec_out, r.vz.at[pl.ds(z, 1)], r.vt.at[pl.ds(a - 1, 1)], p.device(z, p.q))
     run(emit, 0, nb)
     r.gup[...] = uncut(up.land())
     r.gdown[...] = down.land()
     r.gheads[...] = uncut(heads.land())
     r.gback[...] = back.land()
-    arrived(vec_out)
+    copies.arrived(vec_out)
     r.gvec[...] = r.vz[pl.ds(p.z, 1), :] + jnp.sum(r.vt[...], axis=0, keepdims=True)
     copies.finish()
 
@@ -680,7 +739,7 @@
         vec=v((2, QUAD, Z, 128), F32), pick=v((sum(sum_widths(D, FF)), 128), BF16),
         vs=v((2, QUAD, Z, 128), F32), vr=v((QUAD, Z, 128), F32), va=v((QUAD, Z, 128), F32),
         vx=v((QUAD - 1, Z, 128), F32), vz=v((Z, 128), F32), vt=v((Z - 1, 128), F32),
-        local=pltpu.SemaphoreType.DMA((14,)), send=pltpu.SemaphoreType.DMA((72,)), recv=pltpu.SemaphoreType.DMA((72,)),
+        local=pltpu.SemaphoreType.DMA((14,)), send=pltpu.SemaphoreType.DMA((30,)), recv=pltpu.SemaphoreType.DMA((30,)),
     )
     for name, lane, width, own, offset in segments(n, D, FF):
         space[name] = v((1, width), F32)
@@ -747,9 +806,10 @@
         lax.fori_loop(0, nb, step, 0)
 
     set_up(r)
-    for f in (enter, backbone, gates, norms, feed_up, feed_down, emit):
+    for f in (enter, backbone, gates, norms):
         run(f)
-    run(gates_back, True)
+    middle(r, dims, {})
+    run(emit)
     run(leave, True)
     r.gdown[...] = r.dwd_t[...].T
     sums, at = column_sums(r), 0

time: 51.4 us -> 49.9 us (0.971)
  Pallas kernels: 50.4 us -> 48.9 us
    pallas_call x1, Pallas kernels: 48.4 us -> 47 us  [quick(): pl.pallas_call(functools.partial(mega, INPUTS + OUTPUTS + tuple(space), (...]
where the time goes in v4:
time: 49.9 us; the launch traced here: 49.8 us
  Pallas kernels  48.9 us (98%)
  between operations  0.82 us (2%)
    pallas_call x1, Pallas kernels, quick(): pl.pallas_call(functools.partial(mega, INPUTS + OUTPUTS + tuple(space), (...  47 us
    pallas_call x1, Pallas kernels, hand_over(): pl.pallas_call(functools.partial(hand_over_kernel, widths), out_shape=sha...  1.93 us

profile of v4, /device:TPU:0, one launch (start us, length us, event | category | flops | bytes accessed | tf_op | source)
XLA Modules:
  0.0 49.8 jit_solution(6205673181815811610)
XLA Ops:
  0.7 47.0 %shard_map.254 = (bf16[2048,256]{1,0:T(8,128)(2,1)S(1)}, bf16[2048,256]{1,0:T(8,128)(2,1)S(1)}, f32[16,256]{1,0:T(8,128)S(1)}, f32[8,768]{1,0:T(8,128)S(1)}, f32...) custom-call(s32[2]{0:T(128)} %refs_0_.1, bf16[2048,256]{1,0:T(8,128)(2,1)} %refs_1_.1, ...), custom_call_target="tpu_custom_call" | custom-call | tf_op jit(solution)/shard_map/pallas_call | solution.py:757
  47.7 1.9 %shard_map.255 = (bf16[2048,256]{1,0:T(8,128)(2,1)}, bf16[2048,256]{1,0:T(8,128)(2,1)}, f32[16,256]{1,0:T(8,128)}, f32[8,768]{1,0:T(8,128)}, f32[8,1024]{1,0:T(8...) custom-call(bf16[2048,256]{1,0:T(8,128)(2,1)S(1)} %get-tuple-element, ...), custom_call_target="tpu_custom_call" | custom-call | tf_op jit(solution)/shard_map/pallas_call | solution.py:787

commit v5 on v4

--- a/solution.py
+++ b/solution.py
@@ -1,4 +1,5 @@
 import functools
+
 import jax
 import jax.numpy as jnp
 from jax import lax
@@ -25,10 +26,6 @@
 
 def mm_nt(a, b):
     return lax.dot_general(a, b, (((1,), (1,)), ((), ())), preferred_element_type=F32)
-
-
-def mm_tn(a, b):
-    return lax.dot_general(a, b, (((0,), (0,)), ((), ())), preferred_element_type=F32)
 
 
 def shuffle(transposed=False):
@@ -112,12 +109,10 @@
     v = jnp.tanh(heads[:, D : 2 * D])
     f = jnp.tanh(heads[:, 2 * D :])
     keep = 1.0 - o
-    gap = v - f
-    drive = f + o * gap
+    drive = f + o * (v - f)
     r.keep[rows, :] = keep
-    r.to_value[rows, :] = o * (1.0 - v * v)
-    r.to_fallback[rows, :] = keep * (1.0 - f * f)
-    bend = o * keep
+    r.v[rows, :] = v
+    r.f[rows, :] = f
     one = jnp.ones((8, D), F32)
     for s in range(S):
         k = [keep[s * BLK + 8 * j : s * BLK + 8 * j + 8] for j in range(STEPS)]
@@ -135,19 +130,17 @@
         ends = Q + A * carry
         r.scarry[s] = jnp.broadcast_to(ends[7:8], (8, D))
         Q = jnp.where(sub == 0, carry, pltpu.roll(ends, 1, 0))
+        r.start[i, s] = Q
         for j in range(STEPS):
             at = s * BLK + 8 * j
             place = pl.ds(pl.multiple_of(i * (S * BLK) + at, 8), 8)
-            r.to_rate[place, :] = bend[at : at + 8] * (gap[at : at + 8] - Q)
             Q = k[j] * Q + d[j]
             r.state[place, :] = Q
 
 
 def normalise(values, D):
-    mean = jnp.sum(values, axis=1, keepdims=True) * (1.0 / D)
-    c = values - mean
-    var = jnp.sum(c * c, axis=1, keepdims=True) * (1.0 / D)
-    rs = lax.rsqrt(var + 1e-05)
+    c = values - jnp.sum(values, axis=1, keepdims=True) * (1.0 / D)
+    rs = lax.rsqrt(jnp.sum(c * c, axis=1, keepdims=True) + 1e-05 * D)
     return c * rs, rs
 
 
@@ -195,7 +188,7 @@
     total[...] += fold(dx)
     by_gain[...] += fold(ex)
     m1 = jnp.sum(dx, axis=1, keepdims=True) * (1.0 / D)
-    m2 = jnp.sum(ex, axis=1, keepdims=True) * (1.0 / D)
+    m2 = jnp.sum(ex, axis=1, keepdims=True)
     return rs * (dx - m1 - xhat * m2)
 
 
@@ -241,7 +234,14 @@
             H = k[j] * out[j]
         gs += out
     gs = jnp.concatenate(gs, axis=0)
-    gph = jnp.concatenate([gs * r.to_rate[rows, :], gs * r.to_value[rows, :], gs * r.to_fallback[rows, :]], axis=1).astype(BF16)
+    before = []
+    for s in range(S):
+        before += [r.start[i, s], r.state[pl.ds(pl.multiple_of(i * (S * BLK) + s * BLK, BLK), BLK - 8), :]]
+    before = jnp.concatenate(before, axis=0)
+    v, f = r.v[rows, :], r.f[rows, :]
+    go = gs * (1.0 - keep)
+    grate = go * keep * (v - f - before)
+    gph = jnp.concatenate([grate, go * (1.0 - v * v), (gs - go) * (1.0 - f * f)], axis=1).astype(BF16)
     gpb = (mm_nt(gph, r.wh[...]) * r.bend[rows, :]).astype(BF16)
     r.gpb[rows, :] = gpb
     part = mm(r.feat_t[:, rows], gph)
@@ -319,6 +319,8 @@
         else:
             part = jnp.sum(getattr(r, name)[...], axis=0, keepdims=True)
             gain = {"gg1": r.g1, "gb1": r.g1, "gg2": r.g2, "gb2": r.g2}.get(name)
+            if name in ("gg1", "gg2"):
+                part = part * part.shape[1] ** 0.5
             parts.append(part if gain is None else part / gain[...])
     return jnp.concatenate(parts, axis=1)
 
@@ -334,7 +336,7 @@
         joined=v((T, 2 * D), BF16), joined_t=v((2 * D + 16, T), BF16), mixed_cot=v((T, D), BF16),
         half=v((T, D), BF16), half_t=v((D, T), BF16), bend=v((T, D), F32),
         feat=v((T, D), BF16), feat_t=v((D + 16, T), BF16), keep=v((T, D), F32),
-        to_rate=v((T, D), F32), to_value=v((T, D), F32), to_fallback=v((T, D), F32), state=v((T, D), F32),
+        v=v((T, D), F32), f=v((T, D), F32), state=v((T, D), F32), gnorm=v((T, D), F32), start=v((L // BLK, S, 8, D), F32),
         xcarry=v((S, 8, D), F32), scarry=v((S, 8, D), F32), xhat1=v((T, D), F32), xhat2=v((T, D), F32),
         rs1=v((T, 1), F32), rs2=v((T, 1), F32), mid=v((T, D), F32), normed=v((T, D), BF16),
         normed_t=v((D + 16, T), BF16), hidden=v((T, FF), BF16), slope=v((2, S * BLK, FF), F32),
@@ -358,7 +360,7 @@
     r = Refs()
     for name, ref in zip(names, refs):
         setattr(r, name, ref)
-    r.gnorm, r.gmid, r.gpb = r.state, r.xhat2, r.feat
+    r.gmid, r.gpb = r.xhat2, r.feat
     return r
 
 
@@ -417,8 +419,8 @@
 
 
 class Gather:
-    def __init__(self, ref, copies, place):
-        self.ref, self.copies, self.p = ref, copies, place
+    def __init__(self, ref, copies, place, early):
+        self.ref, self.copies, self.p, self.early = ref, copies, place, early
 
     def begin(self, own):
         ref, p = self.ref, self.p
@@ -426,14 +428,14 @@
         self.second = self.copies.group(ref.at[:, pl.ds(0, QUAD - 1), p.c])
         for a in range(1, p.planes):
             self.copies.start(self.first, own, ref.at[p.z, p.q, p.c], p.device(p.plane(a), p.q))
-        for b in range(1, QUAD):
+        for b in range(1, QUAD if self.early else 1):
             self.copies.start(self.second, own, ref.at[p.z, p.q, p.c], p.device(p.z, p.corner(b)))
 
     def spread(self):
         ref, p = self.ref, self.p
         self.copies.arrived(self.first)
-        for a in range(1, p.planes):
-            part = ref.at[p.plane(a), p.q, p.c]
+        parts = [ref.at[p.plane(a), p.q, p.c] for a in range(1, p.planes)] if self.early else [ref.at[:, p.q, p.c]]
+        for part in parts:
             for b in range(1, QUAD):
                 self.copies.start(self.second, part, part, p.device(p.z, p.corner(b)))
 
@@ -573,15 +575,14 @@
         r.pick[pl.ds(lane, width), :] = jnp.where(place == k, 1.0, 0.0).astype(BF16)
 
 
-def owners(n, D, FF):
-    parts, Z = [], n // (2 * QUAD)
+def fill_owned(r, n, D, FF):
+    Z = n // (2 * QUAD)
     for name, lane, width, own, offset in segments(n, D, FF):
         l = lax.broadcasted_iota(jnp.int32, (n, width), 1).astype(F32)
         row = lax.broadcasted_iota(jnp.int32, (n, width), 0)
         z, q, c = row % Z, row // Z % QUAD, row // (Z * QUAD)
         device = ((z * QUAD + q) * 2 + c).astype(F32)
-        parts.append(jnp.floor((l + 0.5) * (1.0 / own)) == device)
-    return jnp.concatenate(parts, axis=1)
+        r.owned[:, pl.ds(lane, width)] = jnp.where(jnp.floor((l + 0.5) * (1.0 / own)) == device, 1.0, 0.0)
 
 
 ROWS = ("gback", "gheads", "gup", "gdown", "gvec")
@@ -619,7 +620,10 @@
     ]
     for load in loads:
         load.start()
-    wb, wh, wu, wd = (Gather(ref, copies, p) for ref in (r.wb, r.wh_cut, r.wu_cut, r.wd))
+    wb, wh, wu, wd = (
+        Gather(ref, copies, p, early)
+        for ref, early in zip((r.wb, r.wh_cut, r.wu_cut, r.wd), (True, True, False, False))
+    )
     vec = GatherRows(r.vec, copies, p)
     pl.semaphore_wait(barrier, len(p.peers()))
     wb.begin(r.wb_own)
@@ -636,15 +640,16 @@
     vec.begin()
     wh.begin(r.wh_cut.at[p.z, p.q, p.c])
     set_up(r)
+    for load in loads[-4:]:
+        load.wait()
+    run(enter, 0, nb)
     wb.spread()
     vec.spread()
     wh.spread()
     wu.begin(r.wu_cut.at[p.z, p.q, p.c])
     wd.begin(r.wd_own)
-    for load in loads[-4:]:
-        load.wait()
-    run(enter, 0, nb)
     fill_pick(r, n, D, FF)
+    fill_owned(r, n, D, FF)
     wb.pair()
     vec.pair()
     wu.spread()
@@ -652,9 +657,10 @@
     wb.end()
     vec.end()
     spread = mm_nt(r.vec[...].reshape(n, 128).astype(BF16), r.pick[...])
-    vectors = jnp.sum(jnp.where(owners(n, D, FF), spread, 0.0), axis=0, keepdims=True)
+    vectors = jnp.sum(r.owned[...] * spread, axis=0, keepdims=True)
     for name, lane, width, own, offset in segments(n, D, FF):
-        getattr(r, name)[...] = vectors[:, lane : lane + width]
+        held = vectors[:, lane : lane + width]
+        getattr(r, name)[...] = held * D**0.5 if name in ("g1", "g2") else held
 
     run(backbone, 0, nb)
     wh.pair()
@@ -683,7 +689,7 @@
     heads.pair()
     back.pair()
 
-    rest, rows = jnp.where(owners(n, D, FF), column_sums(r), 0.0), None
+    rest, rows = r.owned[...] * column_sums(r), None
     for _ in range(3):
         part = rest.astype(BF16)
         rest = rest - part.astype(F32)
@@ -737,6 +743,7 @@
         wh_cut=v((Z, QUAD, 2, 2 * rh, 3 * D // 2), BF16), wu_cut=v((Z, QUAD, 2, 2 * ru, FF // 2), BF16),
         wh=v((D, 3 * D), BF16), wu=v((D, FF), BF16), wh_mine=v((rh, 3 * D), BF16), wu_mine=v((ru, FF), BF16),
         vec=v((2, QUAD, Z, 128), F32), pick=v((sum(sum_widths(D, FF)), 128), BF16),
+        owned=v((n, sum(sum_widths(D, FF))), F32),
         vs=v((2, QUAD, Z, 128), F32), vr=v((QUAD, Z, 128), F32), va=v((QUAD, Z, 128), F32),
         vx=v((QUAD - 1, Z, 128), F32), vz=v((Z, 128), F32), vt=v((Z - 1, 128), F32),
         local=pltpu.SemaphoreType.DMA((14,)), send=pltpu.SemaphoreType.DMA((30,)), recv=pltpu.SemaphoreType.DMA((30,)),
@@ -766,16 +773,16 @@
 
 
 def hand_over_kernel(widths, *refs):
-    count = 6
-    sources, vec, targets = refs[:count], refs[count], refs[count + 1 : 2 * count + 1]
-    smalls, sem = refs[2 * count + 1 : -1], refs[-1]
-    moves = [pltpu.make_async_copy(s, t, sem.at[k]) for k, (s, t) in enumerate(zip(sources, targets))]
+    count, small = 6, len(widths)
+    sources, vec, targets = refs[:count], refs[count], refs[count + 1 : 2 * count + 1 + small]
+    rows, sem = refs[2 * count + 1 + small : -1], refs[-1]
+    at = 0
+    for row, width in zip(rows, widths):
+        row[...] = pltpu.roll(vec[...], (128 - at) % 128, 1)[:, :width]
+        at += width
+    moves = [pltpu.make_async_copy(s, t, sem.at[k]) for k, (s, t) in enumerate(zip(sources + rows, targets))]
     for move in moves:
         move.start()
-    at = 0
-    for small, width in zip(smalls, widths):
-        small[...] = pltpu.roll(vec[...], (128 - at) % 128, 1)[:, :width]
-        at += width
     for move in moves:
         move.wait()
 
@@ -788,8 +795,8 @@
         functools.partial(hand_over_kernel, widths),
         out_shape=shapes,
         in_specs=[vmem] * 7,
-        out_specs=[hbm] * 6 + [vmem] * len(widths),
-        scratch_shapes=[pltpu.SemaphoreType.DMA((6,))],
+        out_specs=[hbm] * len(shapes),
+        scratch_shapes=[pltpu.VMEM((1, w), F32) for w in widths] + [pltpu.SemaphoreType.DMA((len(shapes),))],
         compiler_params=pltpu.CompilerParams(vmem_limit_bytes=16 << 20),
     )(*results)
 
@@ -824,6 +831,8 @@
     T, D = x.shape
     L, FF = T // S, matrices[2].shape[1]
     space = work_space(S, L, D, FF)
+    rows = [v.astype(F32).reshape(1, -1) for v in vectors]
+    rows[2], rows[4] = rows[2] * D**0.5, rows[4] * D**0.5
     names = ("lengths", "x", "cot", "wb", "wh", "wu", "wd", "bb", "bh", "g1", "b1", "g2", "b2", "bu", "bd")
     names += ("out", "ig", "dwb", "dwh", "dwu", "gdown") + tuple("all" + name for name in SUMS) + tuple(space)
     row = lambda a, b: jax.ShapeDtypeStruct((a, b), F32)
@@ -837,7 +846,7 @@
         out_specs=[vmem] * len(shapes),
         scratch_shapes=list(space.values()),
         compiler_params=pltpu.CompilerParams(vmem_limit_bytes=62 << 20),
-    )(lengths, x, cot, *matrices, *(v.astype(F32).reshape(1, -1) for v in vectors))
+    )(lengths, x, cot, *matrices, *rows)
 
 
 def by_collectives(lengths, x, cot, matrices, vectors):

time: 49.9 us -> 49 us (0.982)
  Pallas kernels: 48.9 us -> 48.1 us
where the time goes in v5:
time: 49 us; the launch traced here: 48.9 us
  Pallas kernels  48.1 us (98%)
  between operations  0.82 us (2%)
    pallas_call x1, Pallas kernels, quick(): pl.pallas_call(functools.partial(mega, INPUTS + OUTPUTS + tuple(space), (...  46.6 us
    pallas_call x1, Pallas kernels, hand_over(): pl.pallas_call(functools.partial(hand_over_kernel, widths), out_shape=sha...  1.48 us

profile of v5, /device:TPU:0, one launch (start us, length us, event | category | flops | bytes accessed | tf_op | source)
XLA Modules:
  0.0 48.9 jit_solution(18028508679741536552)
XLA Ops:
  0.7 46.6 %shard_map.254 = (bf16[2048,256]{1,0:T(8,128)(2,1)S(1)}, bf16[2048,256]{1,0:T(8,128)(2,1)S(1)}, f32[16,256]{1,0:T(8,128)S(1)}, f32[8,768]{1,0:T(8,128)S(1)}, f32...) custom-call(s32[2]{0:T(128)} %refs_0_.1, bf16[2048,256]{1,0:T(8,128)(2,1)} %refs_1_.1, ...), custom_call_target="tpu_custom_call" | custom-call | tf_op jit(solution)/shard_map/pallas_call | solution.py:764
  47.2 1.5 %shard_map.255 = (bf16[2048,256]{1,0:T(8,128)(2,1)}, bf16[2048,256]{1,0:T(8,128)(2,1)}, f32[16,256]{1,0:T(8,128)}, f32[8,768]{1,0:T(8,128)}, f32[8,1024]{1,0:T(8...) custom-call(bf16[2048,256]{1,0:T(8,128)(2,1)S(1)} %get-tuple-element, ...), custom_call_target="tpu_custom_call" | custom-call | tf_op jit(solution)/shard_map/pallas_call | solution.py:794
